TPU v7x, 32 devices: a whole 2x2x4 slice. The times are simulated.
32 devices in a mesh: dp: 8 (over z, y), tensor: 4 (over x, core).
Axes of the slice: x: 2, y: 2, z: 4, core: 2. Of those that a mesh axis runs over, the one named last changes fastest.
Arguments:
- block_input: bfloat16 [7680, 1536], P('dp'), may hold values from -6 to 6
- norm1_gain: float32 [1536], replicated, may hold values from 0.1 to 1.9
- query_weight: bfloat16 [1536, 1536], P(None, 'tensor'), may hold values from -0.15625 to 0.15625
- keyvalue_weight: bfloat16 [1536, 256], replicated, may hold values from -0.15625 to 0.15625
- out_weight: bfloat16 [1536, 1536], P('tensor'), may hold values from -0.625 to 0.625
- norm2_gain: float32 [1536], replicated, may hold values from 0.1 to 1.9
- gate_up_weight: bfloat16 [2, 1536, 4608], P(None, None, 'tensor'), may hold values from -0.15625 to 0.15625
- down_weight: bfloat16 [4608, 1536], P('tensor'), may hold values from -0.1875 to 0.1875
- cotangent: bfloat16 [7680, 1536], P('dp'), may hold values from -6 to 6
Outputs:
- block_output: bfloat16 [7680, 1536], P('dp')
- input_grad: bfloat16 [7680, 1536], P('dp')
- norm1_grad: float32 [1536], replicated
- query_grad: float32 [1536, 1536], P(None, 'tensor')
- keyvalue_grad: float32 [1536, 256], replicated
- out_grad: float32 [1536, 1536], P('tensor')
- norm2_grad: float32 [1536], replicated
- gate_up_grad: float32 [2, 1536, 4608], P(None, None, 'tensor')
- down_grad: float32 [4608, 1536], P('tensor')
All inputs are finite; a program needn't handle non-finite values.
Results may differ from a plain program's by a relative error of at most 0.025.
Values may be sent and summed in bfloat16 or wider, within the bound.
No kernel may reach another device: no remote copies, remote signals or barrier semaphores. Data moves between devices by JAX's collectives and lax.ppermute only.
A program may use at most 192 MiB of HBM per device.

v0:
```python
import math

import jax
import jax.numpy as jnp
from jax import lax
from jax.sharding import PartitionSpec as P

WINDOW = 1024


EPSILON = 1e-06
GELU_COEF = 0.7978845608028654


def rms_scale(field, gain):
    factor = lax.rsqrt(jnp.mean(field * field, axis=-1, keepdims=True) + EPSILON)
    return field * factor * gain


def gelu_tanh(field):
    return 0.5 * field * (1.0 + jnp.tanh(GELU_COEF * (field + 0.044715 * field * field * field)))


def geglu(gate_part, up_part):
    return gelu_tanh(gate_part) * up_part


def rope_tables(length, width):
    half_width = width // 2
    position = jnp.arange(length, dtype=jnp.float32)[:, None]
    frequency = jnp.exp(
        jnp.arange(half_width, dtype=jnp.float32) * (-2.0 * math.log(10000.0) / width)
    )
    angle = position * frequency[None, :]
    return (jnp.cos(angle), jnp.sin(angle))


def rotate(field, cosine, sine):
    half_width = field.shape[-1] // 2
    first_half = field[..., :half_width]
    second_half = field[..., half_width:]
    return jnp.concatenate(
        [first_half * cosine - second_half * sine, second_half * cosine + first_half * sine],
        axis=-1,
    )


def rotate_back(field, cosine, sine):
    half_width = field.shape[-1] // 2
    first_half = field[..., :half_width]
    second_half = field[..., half_width:]
    return jnp.concatenate(
        [first_half * cosine + second_half * sine, second_half * cosine - first_half * sine],
        axis=-1,
    )


def product(left, right):
    return jnp.dot(left, right, preferred_element_type=jnp.float32)


def product_left_t(left, right):
    return lax.dot_general(
        left, right, (((0,), (0,)), ((), ())), preferred_element_type=jnp.float32
    )


def product_right_t(left, right):
    return lax.dot_general(
        left, right, (((1,), (1,)), ((), ())), preferred_element_type=jnp.float32
    )


def window_scores(rot_q, rot_k, allowed):
    scores = jnp.einsum("qhd,kd->hqk", rot_q, rot_k, preferred_element_type=jnp.float32)
    return jnp.where(allowed[None], scores, -1e30)


def local(
    block_input,
    norm1_gain,
    query_weight,
    keyvalue_weight,
    out_weight,
    norm2_gain,
    gate_up_weight,
    down_weight,
    cotangent,
):
    length = block_input.shape[0]
    head_dim = keyvalue_weight.shape[1] // 2
    local_heads = query_weight.shape[1] // head_dim
    q_scale = 1.0 / math.sqrt(head_dim)
    cosine, sine = rope_tables(length, head_dim)
    cos_heads = cosine[:, None, :]
    sin_heads = sine[:, None, :]
    row_pos = jnp.arange(length)[:, None]
    col_pos = jnp.arange(length)[None, :]
    allowed = (col_pos <= row_pos) & (row_pos - col_pos < WINDOW)
    input_full = block_input.astype(jnp.float32)
    normed1 = rms_scale(input_full, norm1_gain).astype(jnp.bfloat16)
    queries = product(normed1, query_weight).reshape(length, local_heads, head_dim)
    rot_q = (rotate(queries, cos_heads, sin_heads) * q_scale).astype(jnp.bfloat16)
    keyvalue = product(normed1, keyvalue_weight)
    rot_k = rotate(keyvalue[:, :head_dim], cosine, sine).astype(jnp.bfloat16)
    values = keyvalue[:, head_dim:].astype(jnp.bfloat16)
    scores = window_scores(rot_q, rot_k, allowed)
    row_max = jnp.max(scores, axis=-1, keepdims=True)
    weights = jnp.exp(scores - row_max)
    row_total = jnp.sum(weights, axis=-1, keepdims=True)
    log_total = row_max + jnp.log(row_total)
    probs_low = (weights / row_total).astype(jnp.bfloat16)
    head_out = jnp.einsum("hqk,kd->qhd", probs_low, values, preferred_element_type=jnp.float32)
    head_out = head_out.astype(jnp.bfloat16).reshape(length, local_heads * head_dim)
    attended = lax.psum(product(head_out, out_weight).astype(jnp.bfloat16), "tensor").astype(
        jnp.float32
    )
    residual = input_full + attended
    normed2 = rms_scale(residual, norm2_gain).astype(jnp.bfloat16)
    gate_part = product(normed2, gate_up_weight[0])
    up_part = product(normed2, gate_up_weight[1])
    hidden = geglu(gate_part, up_part).astype(jnp.bfloat16)
    ffn_out = lax.psum(product(hidden, down_weight).astype(jnp.bfloat16), "tensor").astype(
        jnp.float32
    )
    block_output = (residual + ffn_out).astype(jnp.bfloat16)
    down_grad = product_left_t(hidden, cotangent)
    d_hidden = product_right_t(cotangent, down_weight)
    unused_out, geglu_pull = jax.vjp(geglu, gate_part, up_part)
    d_gate, d_up = geglu_pull(d_hidden)
    d_gate = d_gate.astype(jnp.bfloat16)
    d_up = d_up.astype(jnp.bfloat16)
    gate_up_grad = jnp.stack([product_left_t(normed2, d_gate), product_left_t(normed2, d_up)])
    d_normed2_part = product_right_t(d_gate, gate_up_weight[0]) + product_right_t(
        d_up, gate_up_weight[1]
    )
    d_normed2 = lax.psum(d_normed2_part.astype(jnp.bfloat16), "tensor").astype(jnp.float32)
    unused_norm, second_pull = jax.vjp(rms_scale, residual, norm2_gain)
    d_resid_norm, norm2_grad = second_pull(d_normed2)
    d_residual = cotangent.astype(jnp.float32) + d_resid_norm
    d_res_low = d_residual.astype(jnp.bfloat16)
    out_grad = product_left_t(head_out, d_res_low)
    d_heads = (
        product_right_t(d_res_low, out_weight)
        .astype(jnp.bfloat16)
        .reshape(length, local_heads, head_dim)
    )
    scores_again = window_scores(rot_q, rot_k, allowed)
    probs = jnp.exp(scores_again - log_total)
    probs_again = probs.astype(jnp.bfloat16)
    d_probs = jnp.einsum("qhd,kd->hqk", d_heads, values, preferred_element_type=jnp.float32)
    delta = jnp.sum(probs * d_probs, axis=-1, keepdims=True)
    d_scores = (probs * (d_probs - delta)).astype(jnp.bfloat16)
    d_rot_q = jnp.einsum("hqk,kd->qhd", d_scores, rot_k, preferred_element_type=jnp.float32)
    d_rot_k = jnp.einsum("hqk,qhd->kd", d_scores, rot_q, preferred_element_type=jnp.float32)
    d_values = jnp.einsum("hqk,qhd->kd", probs_again, d_heads, preferred_element_type=jnp.float32)
    d_queries = rotate_back(d_rot_q * q_scale, cos_heads, sin_heads).astype(jnp.bfloat16)
    d_queries = d_queries.reshape(length, local_heads * head_dim)
    d_keyvalue = jnp.concatenate([rotate_back(d_rot_k, cosine, sine), d_values], axis=1).astype(
        jnp.bfloat16
    )
    query_grad = product_left_t(normed1, d_queries)
    keyvalue_part = product_left_t(normed1, d_keyvalue)
    d_normed1_part = product_right_t(d_queries, query_weight) + product_right_t(
        d_keyvalue, keyvalue_weight
    )
    d_normed1, keyvalue_grad = (
        lax.psum(d_normed1_part.astype(jnp.bfloat16), "tensor").astype(jnp.float32),
        lax.psum(keyvalue_part.astype(jnp.bfloat16), "tensor").astype(jnp.float32),
    )
    unused_first, first_pull = jax.vjp(rms_scale, input_full, norm1_gain)
    d_input_norm, norm1_grad = first_pull(d_normed1)
    input_grad = (d_residual + d_input_norm).astype(jnp.bfloat16)
    part_one, part_query, part_keyvalue, part_out, part_two, part_gate_up, part_down = (
        lax.psum_scatter(norm1_grad, "dp", scatter_dimension=0, tiled=True),
        lax.psum_scatter(query_grad, "dp", scatter_dimension=0, tiled=True),
        lax.psum_scatter(keyvalue_grad, "dp", scatter_dimension=0, tiled=True),
        lax.psum_scatter(out_grad, "dp", scatter_dimension=1, tiled=True),
        lax.psum_scatter(norm2_grad, "dp", scatter_dimension=0, tiled=True),
        lax.psum_scatter(gate_up_grad, "dp", scatter_dimension=1, tiled=True),
        lax.psum_scatter(down_grad, "dp", scatter_dimension=1, tiled=True),
    )
    norm1_grad, query_grad, keyvalue_grad, out_grad, norm2_grad, gate_up_grad, down_grad = (
        lax.all_gather(part_one.astype(jnp.bfloat16), "dp", axis=0, tiled=True).astype(
            part_one.dtype
        ),
        lax.all_gather(part_query.astype(jnp.bfloat16), "dp", axis=0, tiled=True).astype(
            part_query.dtype
        ),
        lax.all_gather(part_keyvalue.astype(jnp.bfloat16), "dp", axis=0, tiled=True).astype(
            part_keyvalue.dtype
        ),
        lax.all_gather(part_out.astype(jnp.bfloat16), "dp", axis=1, tiled=True).astype(
            part_out.dtype
        ),
        lax.all_gather(part_two.astype(jnp.bfloat16), "dp", axis=0, tiled=True).astype(
            part_two.dtype
        ),
        lax.all_gather(part_gate_up.astype(jnp.bfloat16), "dp", axis=1, tiled=True).astype(
            part_gate_up.dtype
        ),
        lax.all_gather(part_down.astype(jnp.bfloat16), "dp", axis=1, tiled=True).astype(
            part_down.dtype
        ),
    )
    return (
        block_output,
        input_grad,
        norm1_grad,
        query_grad,
        keyvalue_grad,
        out_grad,
        norm2_grad,
        gate_up_grad,
        down_grad,
    )


def solution(mesh):
    return jax.shard_map(
        local,
        mesh=mesh,
        in_specs=(
            P("dp", None),
            P(),
            P(None, "tensor"),
            P(),
            P("tensor", None),
            P(),
            P(None, None, "tensor"),
            P("tensor", None),
            P("dp", None),
        ),
        out_specs=(
            P("dp", None),
            P("dp", None),
            P(),
            P(None, "tensor"),
            P(),
            P("tensor", None),
            P(),
            P(None, None, "tensor"),
            P("tensor", None),
        ),
        check_vma=False,
    )
```

profile of v0, /device:TPU:0, one launch (start us, length us, event | category | flops | bytes accessed | tf_op | source)
XLA Modules:
  0.0 1269.6 jit_solution(13450903692605141059)
XLA Ops:
  29.3 6.7 fusion.4
  36.0 6.6 fusion.3
  43.2 9.0 fusion.50
  59.6 7.9 fusion.81
  67.5 59.9 %all-reduce.11.cloned.1.call-done = bf16[960,1536]{1,0:T(8,128)(2,1)} async-done(((bf16[960,1536]{1,0:T(8,128)(2,1)}), bf16[960,1536]{1,0:T(8,128)(2,1)}) %all-reduce.11.cloned.1.call-update) | async-done | bytes 2949136 | tf_op jit(solution)/shard_map/psum | solution.py:115
  133.1 7.6 fusion.35
  140.7 9.6 multiply_convert_fusion.2
  160.6 7.3 convolution_convert_fusion
  167.9 57.4 %all-reduce.13.cloned.1.call-done = bf16[960,1536]{1,0:T(8,128)(2,1)} async-done(((bf16[960,1536]{1,0:T(8,128)(2,1)}), bf16[960,1536]{1,0:T(8,128)(2,1)}) %all-reduce.13.cloned.1.call-update) | async-done | bytes 2949136 | tf_op jit(solution)/shard_map/psum | solution.py:137
  225.3 6.1 fusion.12
  242.7 8.1 fusion.54
  250.8 9.1 fusion
  260.0 6.7 fusion.2
  291.4 7.1 fusion.42
  298.6 9.7 fusion.83
  308.7 10.0 convolution_bitcast_fusion
  318.7 6.4 convolution_bitcast_fusion.1
  325.1 11.4 pad_maximum_fusion
  336.5 76.4 %all-reduce.15.cloned.1.call-done = (bf16[1536,256]{1,0:T(8,128)(2,1)}, bf16[960,1536]{1,0:T(8,128)(2,1)}, bf16[960,1536]{1,0:T(8,128)(2,1)}) async-done(((bf16[1536,256]{1,0:T(8,128)(2,1)}, bf16[960,1536]{1,0:T(8,128)(2,1)}, bf16[960,1536]{1,0:T(8,128)(2,1)}), (bf16[1536,256]{1,0:T(8,128)(2,1)}, bf16[960,1536]{1,0:T(8,128)(2,1)}, bf16[960,1536]{1,0:T(8,128)(2,1)})) %all-reduce.15.cloned.1.call-update) | async-done | bytes 6684688 | tf_op jit(solution)/shard_map/psum | solution.py:169
  413.0 73.1 %reduce-scatter.6.cloned.1.call-done = f32[192,384]{1,0:T(8,128)} async-done(((f32[1536,384]{1,0:T(8,128)}), f32[192,384]{1,0:T(8,128)}) %reduce-scatter.6.cloned.1.call-update) | async-done | bytes 294928 | tf_op jit(solution)/shard_map/reduce_scatter | solution.py:176
  487.8 70.4 %reduce-scatter.10.cloned.1.call-done = f32[384,192]{0,1:T(8,128)} async-done(((f32[384,1536]{0,1:T(8,128)}), f32[384,192]{0,1:T(8,128)}) %reduce-scatter.10.cloned.1.call-update) | async-done | bytes 294928 | tf_op jit(solution)/shard_map/reduce_scatter | solution.py:178
  559.9 129.9 %reduce-scatter.14.cloned.1.call-done = f32[1152,192]{0,1:T(8,128)} async-done(((f32[1152,1536]{0,1:T(8,128)}), f32[1152,192]{0,1:T(8,128)}) %reduce-scatter.14.cloned.1.call-update) | async-done | bytes 884752 | tf_op jit(solution)/shard_map/reduce_scatter | solution.py:181
  691.9 230.9 %reduce-scatter.12.cloned.1.call-done = f32[2,192,1152]{2,1,0:T(8,128)} async-done(((f32[2,1536,1152]{2,1,0:T(8,128)}), f32[2,192,1152]{2,1,0:T(8,128)}) %reduce-scatter.12.cloned.1.call-update) | async-done | bytes 1769488 | tf_op jit(solution)/shard_map/reduce_scatter | solution.py:180
  931.4 35.2 %all-reduce.4 = (bf16[1536]{0:T(1024)(128)(2,1)S(1)}, bf16[1536]{0:T(1024)(128)(2,1)S(1)}) all-reduce(f32[1536]{0:T(1024)S(1)} %get-tuple-element.38, f32[1536]{0:T(1024)S(1)} %get-tuple-element.36), channel_id=2, replica_groups=mesh['dp'=8,'tensor'=4] {'dp'}, use_global_device_ids=true, to_apply=%region_12.13.clone | all-reduce | flops 3072 | bytes 18432
  967.2 17.7 %all-reduce.5 = (bf16[1536]{0:T(1024)(128)(2,1)S(1)}, bf16[1536]{0:T(1024)(128)(2,1)S(1)}) all-reduce(bf16[1536]{0:T(1024)(128)(2,1)S(1)} %dynamic-update-slice, bf16[1536]{0:T(1024)(128)(2,1)S(1)} %dynamic-update-slice.1), channel_id=1, replica_groups=mesh['dp'=8,'tensor'=4] {'dp'}, use_global_device_ids=true, to_apply=%add | all-reduce | flops 3072 | bytes 12288
  986.1 8.2 fusion.16
  994.3 33.1 %all_gather.23 = bf16[1536,256]{1,0:T(8,128)(2,1)S(1)} all-gather(bf16[192,256]{1,0:T(8,128)(2,1)} %reduce-scatter.8.cloned.1.call-done), channel_id=1, replica_groups=mesh['dp'=8,'tensor'=4] {'dp'}, dimensions={0}, use_global_device_ids=true | all-gather | bytes 884736 | tf_op jit(solution)/shard_map/all_gather | solution.py:190
  1037.2 39.0 %all-gather.7.cloned.1.call-done = bf16[384,1536]{0,1:T(8,128)(2,1)} async-done(((bf16[384,192]{0,1:T(8,128)(2,1)}), bf16[384,1536]{0,1:T(8,128)(2,1)}) %all-gather.7.cloned.1.call-update) | async-done | bytes 1179664 | tf_op jit(solution)/shard_map/all_gather | solution.py:193
  1078.9 64.0 %all-gather.11.cloned.1.call-done = bf16[1152,1536]{0,1:T(8,128)(2,1)} async-done(((bf16[1152,192]{0,1:T(8,128)(2,1)}), bf16[1152,1536]{0,1:T(8,128)(2,1)}) %all-gather.11.cloned.1.call-update) | async-done | bytes 3538960 | tf_op jit(solution)/shard_map/all_gather | solution.py:202
  1142.9 6.0 copy.49
  1148.9 104.0 %all-gather.9.cloned.1.call-done = bf16[2,1536,1152]{2,1,0:T(8,128)(2,1)} async-done(((bf16[2,192,1152]{2,1,0:T(8,128)(2,1)}), bf16[2,1536,1152]{2,1,0:T(8,128)(2,1)}) %all-gather.9.cloned.1.call-update) | async-done | bytes 7077904 | tf_op jit(solution)/shard_map/all_gather | solution.py:199
  1252.9 9.4 convert_element_type.170
  (199 shorter events, 109.0 us)
Async XLA Ops:
  7.2 52.4 %copy-start = (bf16[1152,1536]{1,0:T(8,128)(2,1)S(1)}, bf16[1152,1536]{1,0:T(8,128)(2,1)}, u32[]{:S(2)}) copy-start(bf16[1152,1536]{1,0:T(8,128)(2,1)} %param.16) | copy-start | bytes 10616836
  7.2 120.2 %all-reduce.11.cloned.1.call-start = ((), (), s32[]{:S(2)}) async-start(), calls=%async_computation.5 | async-start | bytes 5898240 | tf_op jit(solution)/shard_map/psum | solution.py:115
  8.5 16.8 %copy-start.46 = (f32[64]{0:T(128)}, f32[64]{0:T(128)S(1)}, u32[]{:S(2)}) copy-start(f32[64]{0:T(128)S(1)} %multiply_exponential_fusion) | copy-start | bytes 772
  11.7 10.5 copy-start.41
  25.3 17.3 %copy-start.21 = (f32[960,256]{1,0:T(8,128)}, f32[960,256]{1,0:T(8,128)S(1)}, u32[]{:S(2)}) copy-start(f32[960,256]{1,0:T(8,128)S(1)} %fusion.77) | copy-start | bytes 2949124
  59.3 166.0 %all-reduce.13.cloned.1.call-start = ((), (), s32[]{:S(2)}) async-start(), calls=%async_computation.6 | async-start | bytes 5898240 | tf_op jit(solution)/shard_map/psum | solution.py:137
  67.5 64.4 %copy-start.32 = (f32[1536]{0:T(1024)S(1)}, f32[1536]{0:T(1024)}, u32[]{:S(2)}) copy-start(f32[1536]{0:T(1024)} %param.14) | copy-start | bytes 18436
  131.9 8.7 slice-start.3
  131.9 8.7 slice-start.5
  159.8 253.2 %all-reduce.15.cloned.1.call-start = ((), (), s32[]{:S(2)}) async-start(), calls=%async_computation.16 | async-start | bytes 13369344 | tf_op jit(solution)/shard_map/psum | solution.py:169
  167.9 63.5 %copy-start.40 = (f32[960]{0:T(1024)S(1)}, f32[960]{0:T(1024)}, u32[]{:S(2)}) copy-start(f32[960]{0:T(1024)} %copy-done.39) | copy-start | bytes 11524
  167.9 63.5 %copy-start.3 = (bf16[960,1536]{1,0:T(8,128)(2,1)S(1)}, bf16[960,1536]{1,0:T(8,128)(2,1)}, u32[]{:S(2)}) copy-start(bf16[960,1536]{1,0:T(8,128)(2,1)} %param.9) | copy-start | bytes 8847364
  167.9 63.5 %copy-start.33 = (f32[1536]{0:T(1024)S(1)}, f32[1536]{0:T(1024)}, u32[]{:S(2)}) copy-start(f32[1536]{0:T(1024)} %param.14) | copy-start | bytes 18436
  167.9 63.5 %copy-start.35 = (f32[960]{0:T(1024)S(1)}, f32[960]{0:T(1024)}, u32[]{:S(2)}) copy-start(f32[960]{0:T(1024)} %copy-done.34) | copy-start | bytes 11524
  242.7 8.2 copy-start.22
  242.7 17.3 %slice-start = ((s8[11796480]{0:T(1024)(128)(4,1)}), s8[4194304]{0:T(1024)(128)(4,1)S(1)}, s32[]{:S(2)}) async-start(s8[11796480]{0:T(1024)(128)(4,1)} %bitcast.109), calls=%async_computation.17 | async-start | bytes 8388608
  242.7 17.3 %slice-start.1 = ((s8[11796480]{0:T(1024)(128)(4,1)}), s8[4194304]{0:T(1024)(128)(4,1)S(1)}, s32[]{:S(2)}) async-start(s8[11796480]{0:T(1024)(128)(4,1)} %bitcast.109), calls=%async_computation.18 | async-start | bytes 8388608
  250.8 9.1 slice-start.2
  286.4 199.8 %reduce-scatter.6.cloned.1.call-start = ((), (), s32[]{:S(2)}) async-start(), calls=%async_computation.7 | async-start | bytes 2654208 | tf_op jit(solution)/shard_map/reduce_scatter | solution.py:176
  291.3 266.9 %reduce-scatter.10.cloned.1.call-start = ((), (), s32[]{:S(2)}) async-start(), calls=%async_computation.10 | async-start | bytes 2654208 | tf_op jit(solution)/shard_map/reduce_scatter | solution.py:178
  298.5 391.3 %reduce-scatter.14.cloned.1.call-start = ((), (), s32[]{:S(2)}) async-start(), calls=%async_computation.14 | async-start | bytes 7962624 | tf_op jit(solution)/shard_map/reduce_scatter | solution.py:181
  308.3 614.4 %reduce-scatter.12.cloned.1.call-start = ((), (), s32[]{:S(2)}) async-start(), calls=%async_computation.12 | async-start | bytes 15925248 | tf_op jit(solution)/shard_map/reduce_scatter | solution.py:180
  308.6 10.0 copy-start.20
  308.6 10.0 copy-start.50
  336.5 588.8 %copy-start.45 = (u32[32]{0:T(128)S(1)}, u32[32]{0:T(128)}, u32[]{:S(2)}) copy-start(u32[32]{0:T(128)} %constant.32) | copy-start | bytes 388
  336.5 657.9 %reduce-scatter.8.cloned.1.call-start = ((), (), s32[]{:S(2)}) async-start(), calls=%async_computation.9 | async-start | bytes 884736 | tf_op jit(solution)/shard_map/reduce_scatter | solution.py:177
  413.0 621.4 %all-gather.5.cloned.1.call-start = ((), (), s32[]{:S(2)}) async-start(), calls=%async_computation.8 | async-start | bytes 1327104 | tf_op jit(solution)/shard_map/all_gather | solution.py:187
  487.8 588.4 %all-gather.7.cloned.1.call-start = ((), (), s32[]{:S(2)}) async-start(), calls=%async_computation.11 | async-start | bytes 1327104 | tf_op jit(solution)/shard_map/all_gather | solution.py:193
  559.9 583.1 %all-gather.11.cloned.1.call-start = ((), (), s32[]{:S(2)}) async-start(), calls=%async_computation.15 | async-start | bytes 3981312 | tf_op jit(solution)/shard_map/all_gather | solution.py:202
  691.8 294.3 %copy-start.38 = (f32[960]{0:T(1024)S(1)}, f32[960]{0:T(1024)}, u32[]{:S(2)}) copy-start(f32[960]{0:T(1024)} %copy-done.37) | copy-start | bytes 11524
  691.8 561.1 %all-gather.9.cloned.1.call-start = ((), (), s32[]{:S(2)}) async-start(), calls=%async_computation.13 | async-start | bytes 7962624 | tf_op jit(solution)/shard_map/all_gather | solution.py:199
  1252.9 9.4 copy-start.1
  (39 other events, 160.5 us)
Sparse Core Ops, SparseCore 0:
  59.4 67.9 all-reduce.10
  159.9 65.3 all-reduce.12
  286.5 126.4 all-reduce.14
  416.9 69.1 reduce-scatter.5
  490.0 68.1 reduce-scatter.9
  561.7 128.0 reduce-scatter.13
  694.5 228.2 reduce-scatter.11
  926.4 61.4 reduce-scatter.7
  990.7 43.6 all-gather.4
  1036.4 39.7 all-gather.6
  1079.0 63.9 all-gather.10
  1145.6 107.2 all-gather.8
where the time goes:
time: 1270 us
  waiting for transfers between devices  911 us (72%)
  matrix products  140 us (11%)
  other arithmetic  86.6 us (7%)
  blocking collectives  86 us (7%)
  local copies, waits for them, and re-layouts  28.7 us (2%)
  between operations  16.7 us (1%)
    reduce_scatter x1, waiting for transfers between devices, local(): lax.psum_scatter(gate_up_grad, 'dp', scatter_dimension=1, tiled=True)  231 us
    reduce_scatter x1, waiting for transfers between devices, local(): lax.psum_scatter(down_grad, 'dp', scatter_dimension=1, tiled=True)  130 us
    all_gather x1, waiting for transfers between devices, local(): lax.all_gather(part_gate_up.astype(jnp.bfloat16), 'dp', axis=1, tiled=True)  104 us
    psum x1, waiting for transfers between devices, local(): lax.psum(keyvalue_part.astype(jnp.bfloat16), 'tensor').astype(jnp.float32)  76.4 us
    reduce_scatter x1, waiting for transfers between devices, local(): lax.psum_scatter(query_grad, 'dp', scatter_dimension=0, tiled=True)  73.1 us
    reduce_scatter x1, waiting for transfers between devices, local(): lax.psum_scatter(out_grad, 'dp', scatter_dimension=1, tiled=True)  70.4 us
    all_gather x1, waiting for transfers between devices, local(): lax.all_gather(part_down.astype(jnp.bfloat16), 'dp', axis=1, tiled=True)  64 us
    psum x1, waiting for transfers between devices, local(): lax.psum(product(head_out, out_weight).astype(jnp.bfloat16), 'tensor')  59.9 us
  transfers between devices with their start and end apart: 12, of which 11 were waited for; matrix products, arithmetic and copies ran while one was open for 8% of the time, Pallas kernels for 0%

commit v1 on v0

v1 whole, which is shorter than its diff:
```python
import math

import jax
import jax.numpy as jnp
import numpy as np
from jax import lax
from jax.sharding import PartitionSpec as P

WINDOW = 1024
EPSILON = 1e-06
GELU_COEF = 0.7978845608028654
BF16 = jnp.bfloat16
F32 = jnp.float32

RING = (0, 2, 4, 6, 7, 5, 3, 1)


def product(left, right):
    return jnp.dot(left, right, preferred_element_type=F32)


def product_left_t(left, right):
    return lax.dot_general(left, right, (((0,), (0,)), ((), ())), preferred_element_type=F32)


def product_right_t(left, right):
    return lax.dot_general(left, right, (((1,), (1,)), ((), ())), preferred_element_type=F32)


def rope_tables(length, width):
    half_width = width // 2
    position = jnp.arange(length, dtype=F32)[:, None]
    frequency = jnp.exp(jnp.arange(half_width, dtype=F32) * (-2.0 * math.log(10000.0) / width))
    angle = position * frequency[None, :]
    return jnp.cos(angle), jnp.sin(angle)


def rotate(field, cosine, sine):
    half_width = field.shape[-1] // 2
    first_half = field[..., :half_width]
    second_half = field[..., half_width:]
    return jnp.concatenate(
        [first_half * cosine - second_half * sine, second_half * cosine + first_half * sine],
        axis=-1,
    )


def rotate_back(field, cosine, sine):
    return rotate(field, cosine, -sine)


def swap_core(field):
    return lax.ppermute(field, "tensor", [(i, i ^ 1) for i in range(4)])


def swap_x(field):
    return lax.ppermute(field, "tensor", [(i, i ^ 2) for i in range(4)])


def own_rows(field, core, half):
    return lax.dynamic_slice_in_dim(field, core * half, half, 0)


def both_halves(own, sibling, core):
    half = own.shape[0]
    out = jnp.zeros((2 * half,) + own.shape[1:], own.dtype)
    out = lax.dynamic_update_slice_in_dim(out, own, core * half, 0)
    return lax.dynamic_update_slice_in_dim(out, sibling, (1 - core) * half, 0)


class Ring:
    def __init__(self, forward):
        order = RING if forward else RING[::-1]
        self.perm = [(order[i], order[(i + 1) % 8]) for i in range(8)]
        place = np.zeros(8, np.int32)
        for i, device in enumerate(order):
            place[device] = i
        self.place = jnp.asarray(place)[lax.axis_index("dp")]

    def all_reduce(self, fields):
        rows = [field.shape[0] // 8 for field in fields]
        cuts = np.cumsum([0] + rows)

        def chunk(k):
            parts = [lax.dynamic_slice_in_dim(f, k * r, r, 0) for f, r in zip(fields, rows)]
            return parts[0] if len(parts) == 1 else jnp.concatenate(parts, 0)

        travelling = chunk((self.place + 7) % 8)
        for step in range(7):
            arrived = lax.ppermute(travelling, "dp", self.perm)
            mine = chunk((self.place + 14 - step) % 8)
            travelling = (arrived.astype(F32) + mine.astype(F32)).astype(BF16)
        outs = [jnp.zeros(f.shape, F32) for f in fields]

        def place_chunk(outs, piece, k):
            return [
                lax.dynamic_update_slice_in_dim(o, piece[a:b].astype(F32), k * r, 0)
                for o, r, a, b in zip(outs, rows, cuts[:-1], cuts[1:])
            ]

        outs = place_chunk(outs, travelling, self.place)
        for step in range(7):
            travelling = lax.ppermute(travelling, "dp", self.perm)
            outs = place_chunk(outs, travelling, (self.place + 7 - step) % 8)
        return outs


class Sum:
    def all_reduce(self, fields):
        return [lax.psum(field, "dp").astype(F32) for field in fields]


def small_sum(field, n_dp):
    if n_dp & (n_dp - 1):
        field = lax.psum(field, "dp")
    else:
        step = 1
        while step < n_dp:
            field = field + lax.ppermute(field, "dp", [(i, i ^ step) for i in range(n_dp)])
            step *= 2
    return field + swap_core(field)


def make_local(n_dp):
    def local(
        block_input,
        norm1_gain,
        query_weight,
        keyvalue_weight,
        out_weight,
        norm2_gain,
        gate_up_weight,
        down_weight,
        cotangent,
    ):
        length, width = block_input.shape
        half = length // 2
        head_dim = keyvalue_weight.shape[1] // 2
        heads = 2 * query_weight.shape[1] // head_dim
        q_scale = 1.0 / math.sqrt(head_dim)
        tensor = lax.axis_index("tensor")
        core = tensor % 2
        chip = tensor // 2
        clockwise, counter = (Ring(True), Ring(False)) if n_dp == 8 else (Sum(), Sum())

        query_chip = jnp.concatenate([query_weight, swap_core(query_weight)], 1)
        out_chip = jnp.concatenate([out_weight, swap_core(out_weight)], 0)

        input_full = block_input.astype(F32)
        factor1 = lax.rsqrt(jnp.mean(input_full * input_full, -1, keepdims=True) + EPSILON)
        normed1 = (input_full * factor1 * norm1_gain).astype(BF16)
        input_own = own_rows(block_input, core, half).astype(F32)
        factor1_own = own_rows(factor1, core, half)
        normed1_own = own_rows(normed1, core, half)
        cosine, sine = rope_tables(length, head_dim)
        cos_own = own_rows(cosine, core, half)[:, None, :]
        sin_own = own_rows(sine, core, half)[:, None, :]

        keyvalue = product(normed1, keyvalue_weight)
        rot_k = rotate(keyvalue[:, :head_dim], cosine, sine).astype(BF16)
        values = keyvalue[:, head_dim:].astype(BF16)
        queries = product(normed1_own, query_chip).reshape(half, heads, head_dim)
        rot_q = (rotate(queries, cos_own, sin_own) * q_scale).astype(BF16)

        row_pos = core * half + jnp.arange(half)[:, None]
        col_pos = jnp.arange(length)[None, :]
        allowed = (col_pos <= row_pos) & (row_pos - col_pos < WINDOW)
        scores = jnp.einsum("qhd,kd->hqk", rot_q, rot_k, preferred_element_type=F32)
        scores = jnp.where(allowed[None], scores, -1e30)
        weights = jnp.exp(scores - jnp.max(scores, axis=-1, keepdims=True))
        probs = weights / jnp.sum(weights, axis=-1, keepdims=True)
        probs_low = probs.astype(BF16)
        head_out = jnp.einsum("hqk,kd->qhd", probs_low, values, preferred_element_type=F32)
        head_out = head_out.astype(BF16).reshape(half, heads * head_dim)

        attn_part = product(head_out, out_chip).astype(BF16)
        attended = attn_part.astype(F32) + swap_x(attn_part).astype(F32)
        residual = input_own + attended
        factor2 = lax.rsqrt(jnp.mean(residual * residual, -1, keepdims=True) + EPSILON)
        normed2_own = (residual * factor2 * norm2_gain).astype(BF16)
        normed2 = both_halves(normed2_own, swap_core(normed2_own), core)

        gate_weight, up_weight = gate_up_weight[0], gate_up_weight[1]
        gate = product(normed2, gate_weight)
        up = product(normed2, up_weight)
        inner = jnp.tanh(GELU_COEF * (gate + 0.044715 * gate * gate * gate))
        gelu = 0.5 * gate * (1.0 + inner)
        slope = 0.5 * (1.0 + inner) + 0.5 * gate * (1.0 - inner * inner) * GELU_COEF * (
            1.0 + 3.0 * 0.044715 * gate * gate
        )
        hidden = (gelu * up).astype(BF16)
        down_grad = product_left_t(hidden, cotangent).astype(BF16)
        d_hidden = product_right_t(cotangent, down_weight)
        d_gate = (d_hidden * up * slope).astype(BF16)
        d_up = (d_hidden * gelu).astype(BF16)
        gate_grad = product_left_t(normed2, d_gate).astype(BF16)
        up_grad = product_left_t(normed2, d_up).astype(BF16)

        middle = width // 2
        (down_left,) = clockwise.all_reduce([down_grad[:, :middle]])
        (down_right,) = counter.all_reduce([down_grad[:, middle:]])
        (gate_sum,) = clockwise.all_reduce([gate_grad])
        (up_sum,) = counter.all_reduce([up_grad])
        down_sum = jnp.concatenate([down_left, down_right], 1)
        gate_up_sum = jnp.stack([gate_sum, up_sum])

        def chip_sum(part):
            mine = own_rows(part, core, half)
            other = own_rows(part, 1 - core, half).astype(BF16)
            on_chip = (mine + swap_core(other).astype(F32)).astype(BF16)
            return on_chip.astype(F32) + swap_x(on_chip).astype(F32)

        d_normed2 = chip_sum(product_right_t(d_gate, gate_weight) + product_right_t(d_up, up_weight))
        scaled = norm2_gain * d_normed2
        norm2_part = jnp.sum(d_normed2 * residual * factor2, axis=0)
        d_residual = (
            cotangent_own(cotangent, core, half)
            + factor2 * scaled
            - residual * factor2**3 * jnp.mean(scaled * residual, -1, keepdims=True)
        )
        d_res_low = d_residual.astype(BF16)
        out_part = product_left_t(head_out, d_res_low)
        own_cols = query_weight.shape[1]
        out_grad = (out_part[:own_cols] + swap_core(out_part[own_cols:].astype(BF16)).astype(F32)).astype(BF16)
        d_heads = product_right_t(d_res_low, out_chip).astype(BF16).reshape(half, heads, head_dim)

        d_probs = jnp.einsum("qhd,kd->hqk", d_heads, values, preferred_element_type=F32)
        delta = jnp.sum(probs * d_probs, axis=-1, keepdims=True)
        d_scores = (probs * (d_probs - delta)).astype(BF16)
        d_rot_q = jnp.einsum("hqk,kd->qhd", d_scores, rot_k, preferred_element_type=F32)
        d_rot_k = jnp.einsum("hqk,qhd->kd", d_scores, rot_q, preferred_element_type=F32)
        d_values = jnp.einsum("hqk,qhd->kd", probs_low, d_heads, preferred_element_type=F32)
        d_queries = rotate_back(d_rot_q * q_scale, cos_own, sin_own).astype(BF16)
        d_queries = d_queries.reshape(half, heads * head_dim)
        d_keyvalue = chip_sum(jnp.concatenate([rotate_back(d_rot_k, cosine, sine), d_values], 1)).astype(BF16)

        query_part = product_left_t(normed1_own, d_queries)
        query_grad = (
            query_part[:, :own_cols] + swap_core(query_part[:, own_cols:].astype(BF16)).astype(F32)
        ).astype(BF16)
        mine = lax.dynamic_slice_in_dim(d_keyvalue, chip * head_dim, head_dim, 1)
        kv_part = product_left_t(normed1_own, mine)
        kv_mine = own_rows(kv_part, core, middle)
        kv_other = own_rows(kv_part, 1 - core, middle).astype(BF16)
        kv_grad = (kv_mine + swap_core(kv_other).astype(F32)).astype(BF16)
        lanes = own_cols // head_dim
        kv_rows = middle // lanes
        kv_wide = jnp.concatenate([kv_grad[i * kv_rows : (i + 1) * kv_rows] for i in range(lanes)], 1)

        (out_sum,) = clockwise.all_reduce([out_grad])
        query_sum, kv_sum = counter.all_reduce([query_grad, kv_wide])

        d_normed1_part = product_right_t(d_queries, query_chip).astype(BF16)
        d_normed1 = (d_normed1_part.astype(F32) + swap_x(d_normed1_part).astype(F32)) + product_right_t(
            d_keyvalue, keyvalue_weight
        )
        scaled1 = norm1_gain * d_normed1
        norm1_part = jnp.sum(d_normed1 * input_own * factor1_own, axis=0)
        input_grad_own = (
            d_residual
            + factor1_own * scaled1
            - input_own * factor1_own**3 * jnp.mean(scaled1 * input_own, -1, keepdims=True)
        ).astype(BF16)
        input_grad = both_halves(input_grad_own, swap_core(input_grad_own), core)

        ffn_out = chip_sum(product(hidden, down_weight))
        output_own = (residual + ffn_out).astype(BF16)
        block_output = both_halves(output_own, swap_core(output_own), core)

        norm_sums = small_sum(jnp.stack([norm1_part, norm2_part]), n_dp)

        kv_tall = jnp.concatenate([kv_sum[:, i * head_dim : (i + 1) * head_dim] for i in range(lanes)], 0).astype(BF16)
        kv_column = both_halves(kv_tall, swap_core(kv_tall), core)
        kv_other_column = swap_x(kv_column)
        kv_out = jnp.zeros(keyvalue_weight.shape, BF16)
        kv_out = lax.dynamic_update_slice_in_dim(kv_out, kv_column, chip * head_dim, 1)
        kv_out = lax.dynamic_update_slice_in_dim(kv_out, kv_other_column, (1 - chip) * head_dim, 1)

        return (
            block_output,
            input_grad,
            norm_sums[0],
            query_sum,
            kv_out.astype(F32),
            out_sum,
            norm_sums[1],
            gate_up_sum,
            down_sum,
        )

    return local


def cotangent_own(cotangent, core, half):
    return own_rows(cotangent, core, half).astype(F32)


def solution(mesh):
    return jax.shard_map(
        make_local(mesh.shape["dp"]),
        mesh=mesh,
        in_specs=(
            P("dp", None),
            P(),
            P(None, "tensor"),
            P(),
            P("tensor", None),
            P(),
            P(None, None, "tensor"),
            P("tensor", None),
            P("dp", None),
        ),
        out_specs=(
            P("dp", None),
            P("dp", None),
            P(),
            P(None, "tensor"),
            P(),
            P("tensor", None),
            P(),
            P(None, None, "tensor"),
            P("tensor", None),
        ),
        check_vma=False,
    )
```

time: 1270 us -> 677 us (0.53)
  waiting for transfers between devices: 911 us -> 265 us
  starting transfers between devices: 1.17 us -> 109 us
  blocking collectives: 86 us -> 0 us
  matrix products: 140 us -> 107 us
  other arithmetic: 86.6 us -> 115 us
  local copies, waits for them, and re-layouts: 28.7 us -> 51.2 us
    reduce_scatter x5 -> x0, waiting for transfers between devices: 504 us -> none  [the longest x1 231 us: local(): lax.psum_scatter(gate_up_grad, 'dp', scatter_dimension=1, tiled=True)]
    ppermute x0 -> x106, waiting for transfers between devices: none -> 265 us  [the longest x42 98.3 us: all_reduce(): travelling = lax.ppermute(travelling, 'dp', self.perm)]
    all_gather x4 -> x0, waiting for transfers between devices: 213 us -> none  [the longest x1 104 us: local(): lax.all_gather(part_gate_up.astype(jnp.bfloat16), 'dp', axis=1, tiled=True)]
    psum x3 -> x0, waiting for transfers between devices: 194 us -> none  [the longest x1 76.4 us: local(): lax.psum(keyvalue_part.astype(jnp.bfloat16), 'tensor').astype(jnp.float32)]
    ppermute x0 -> x106, starting transfers between devices: none -> 109 us  [the longest x42 52.4 us: all_reduce(): arrived = lax.ppermute(travelling, 'dp', self.perm)]
    dynamic_update_slice x0 -> x59, other arithmetic: none -> 55.4 us  [the longest x56 48 us: place_chunk(): lax.dynamic_update_slice_in_dim(o, piece[a:b].astype(F32), k * r, 0)]
    unnamed x2 -> x0, blocking collectives: 52.9 us -> none
    all_gather x1 -> x0, blocking collectives: 33.1 us -> none  [local(): lax.all_gather(part_keyvalue.astype(jnp.bfloat16), 'dp', axis=0, tiled=True)]
  transfers between devices with their start and end apart: 12 -> 106, of which waited for: 11 -> 45; matrix products, arithmetic and copies ran while one was open for 8% -> 33% of each run, Pallas kernels for 0% -> 0%
where the time goes in v1:
time: 677 us; the launch traced here: 672 us
  waiting for transfers between devices  265 us (39%)
  other arithmetic  115 us (17%)
  starting transfers between devices  109 us (16%)
  matrix products  107 us (16%)
  local copies, waits for them, and re-layouts  51.2 us (8%)
  between operations  25.1 us (4%)
    ppermute x42, waiting for transfers between devices, all_reduce(): travelling = lax.ppermute(travelling, 'dp', self.perm)  98.3 us
    ppermute x42, waiting for transfers between devices, all_reduce(): arrived = lax.ppermute(travelling, 'dp', self.perm)  96.7 us
    ppermute x6, waiting for transfers between devices, swap_x(): return lax.ppermute(field, 'tensor', [(i, i ^ 2) for i in range(4)])  56.9 us
    ppermute x42, starting transfers between devices, all_reduce(): arrived = lax.ppermute(travelling, 'dp', self.perm)  52.4 us
    dynamic_update_slice x56, other arithmetic, place_chunk(): lax.dynamic_update_slice_in_dim(o, piece[a:b].astype(F32), k * r, 0)  48 us
    ppermute x42, starting transfers between devices, all_reduce(): travelling = lax.ppermute(travelling, 'dp', self.perm)  41.9 us
    dot_general x6, matrix products, product_right_t(): lax.dot_general(left, right, (((1,), (1,)), ((), ())), preferred_element_...  25.4 us
    dot_general x6, matrix products, product(): return jnp.dot(left, right, preferred_element_type=F32)  24 us
  transfers between devices with their start and end apart: 106, of which 45 were waited for; matrix products, arithmetic and copies ran while one was open for 33% of the time, Pallas kernels for 0%

profile of v1, /device:TPU:0, one launch (start us, length us, event | category | flops | bytes accessed | tf_op | source)
XLA Modules:
  0.0 672.3 jit_solution(7931418017921060242)
XLA Ops:
  29.9 10.4 %fusion.82 = (f32[6,480]{1,0:T(8,128)}, f32[6,480,960]{1,2,0:T(8,128)}) fusion(pred[480,960]{0,1:T(8,128)(4,1)} %fusion.41, bf16[480,6,128]{2,0,1:T(8,128)(2,1)} %fusion.42, bf16[960,64]{1,0:T(8,128)(2,1)} %get-tuple-element.55, bf16[960,64]{1,0:T(8,128)(2,1)} %get-tuple-element.54), kind=kOutput, calls=%fused_computation.285 | convolution fusion | flops 716575680 | bytes 12514560 | tf_op jit(solution)/shard_map/sub | solution.py:170
  40.3 7.8 %fusion.48 = bf16[480,6,128]{2,0,1:T(8,128)(2,1)} fusion(f32[960,256]{1,0:T(8,128)} %fusion.83, f32[6,480,960]{1,2,0:T(8,128)} %get-tuple-element.79, f32[6,480]{1,0:T(8,128)} %get-tuple-element.78), kind=kOutput, calls=%fused_computation.94 | convolution fusion | flops 713687040 | bytes 12795904 | tf_op jit(solution)/shard_map/hqk,kd->qhd/dot_general | solution.py:173
  59.1 32.7 %collective-permute-done.2 = bf16[480,1536]{1,0:T(8,128)(2,1)S(1)} collective-permute-done((bf16[480,1536]{1,0:T(8,128)(2,1)S(1)}, bf16[480,1536]{1,0:T(8,128)(2,1)S(1)}, u32[]{:S(2)}, u32[]{:S(2)}) %collective-permute-start.2) | collective-permute-done | bytes 1474592 | tf_op jit(solution)/shard_map/ppermute | solution.py:57
  124.4 6.0 fusion.85
  135.9 9.3 %multiply_convert_fusion = (bf16[960,1152]{1,0:T(8,128)(2,1)}, bf16[960,1152]{1,0:T(8,128)(2,1)S(1)}, bf16[960,1152]{1,0:T(8,128)(2,1)}) fusion(f32[960,1152]{1,0:T(8,128)S(1)} %fusion.85, f32[960,1152]{1,0:T(8,128)S(1)} %fusion.18, bf16[960,1536]{1,0:T(8,128)(2,1)S(1)} %constant_dynamic-update-slice_fusion.8, bf16[2,1536,1152]{2,1,0:T(8,128)(2,1)S(1)} %bitcast.192), kind=kOutput, calls=%fused_computation.35 | convolution fusion | flops 3425034240 | bytes 21970944 | tf_op jit(solution)/shard_map/dot_general | solution.py:19
  145.2 5.9 fusion.20
  151.0 5.0 convolution_convert_fusion.2
  170.4 8.4 %convolution_add_fusion = f32[960,1536]{1,0:T(8,128)S(1)} fusion(f32[960,1536]{1,0:T(8,128)} %fusion.20, bf16[960,1152]{1,0:T(8,128)(2,1)S(1)} %copy-done.47, bf16[2,1536,1152]{2,1,0:T(8,128)(2,1)} %param.17), kind=kOutput, calls=%fused_computation.38 | convolution fusion | flops 3398860800 | bytes 17547264 | tf_op jit(solution)/shard_map/dot_general | solution.py:27
  183.9 12.7 %collective-permute-done.92 = bf16[144,768]{1,0:T(8,128)(2,1)S(1)} collective-permute-done((bf16[144,768]{1,0:T(8,128)(2,1)S(1)}, bf16[144,768]{1,0:T(8,128)(2,1)S(1)}, u32[]{:S(2)}, u32[]{:S(2)}) %collective-permute-start.92) | collective-permute-done | bytes 221216 | tf_op jit(solution)/shard_map/ppermute | solution.py:90
  198.4 4.8 collective-permute-done.78
  214.6 8.6 %collective-permute-done.94 = bf16[144,768]{1,0:T(8,128)(2,1)S(1)} collective-permute-done((bf16[144,768]{1,0:T(8,128)(2,1)S(1)}, bf16[144,768]{1,0:T(8,128)(2,1)S(1)}, u32[]{:S(2)}, u32[]{:S(2)}) %collective-permute-start.94) | collective-permute-done | bytes 221216 | tf_op jit(solution)/shard_map/ppermute | solution.py:90
  240.9 6.1 collective-permute-done.96
  248.4 5.6 collective-permute-done.82
  257.4 4.9 collective-permute-done.97
  286.8 5.6 collective-permute-done.100
  302.0 4.9 collective-permute-done.101
  310.9 5.0 collective-permute-done.102
  334.2 6.5 collective-permute-done.104
  358.8 11.2 %fusion.1 = (f32[6,480]{1,0:T(8,128)S(1)}, f32[960,480,6]{1,0,2:T(8,128)}) fusion(f32[6,480,960]{1,2,0:T(8,128)} %get-tuple-element.79, f32[6,480]{1,0:T(8,128)S(1)} %copy-done.40, bf16[480,6,128]{0,2,1:T(8,128)(2,1)} %bitcast.185, f32[960,256]{1,0:T(8,128)} %fusion.83), kind=kOutput, calls=%fused_computation.4 | convolution fusion | flops 716080320 | bytes 23910912 | tf_op jit(solution)/shard_map/qhd,kd->hqk/dot_general | solution.py:227
  370.0 6.7 fusion.3
  424.8 6.9 %pad_maximum_fusion.1 = f32[1152,1536]{1,0:T(8,128)} fusion(f32[1152,768]{1,0:T(8,128)} %convert_dynamic-update-slice_fusion.16, f32[1152,768]{1,0:T(8,128)} %convert_dynamic-update-slice_fusion.24), kind=kLoop, calls=%fused_computation.15 | loop fusion | flops 1769472 | bytes 14155776 | tf_op jit(solution)/shard_map/concatenate | solution.py:204
  431.7 14.6 %collective-permute-done.11 = bf16[480,256]{1,0:T(8,128)(2,1)S(1)} collective-permute-done((bf16[480,256]{1,0:T(8,128)(2,1)S(1)}, bf16[480,256]{1,0:T(8,128)(2,1)S(1)}, u32[]{:S(2)}, u32[]{:S(2)}) %collective-permute-start.11) | collective-permute-done | bytes 245792 | tf_op jit(solution)/shard_map/ppermute | solution.py:57
  447.4 10.1 %collective-permute-done.71 = bf16[192,1152]{1,0:T(8,128)(2,1)S(1)} collective-permute-done((bf16[192,1152]{1,0:T(8,128)(2,1)}, bf16[192,1152]{1,0:T(8,128)(2,1)S(1)}, u32[]{:S(2)}, u32[]{:S(2)}) %collective-permute-start.71) | collective-permute-done | bytes 442400 | tf_op jit(solution)/shard_map/ppermute | solution.py:103
  460.3 7.2 %collective-permute-done.57 = bf16[192,1152]{1,0:T(8,128)(2,1)S(1)} collective-permute-done((bf16[192,1152]{1,0:T(8,128)(2,1)S(1)}, bf16[192,1152]{1,0:T(8,128)(2,1)S(1)}, u32[]{:S(2)}, u32[]{:S(2)}) %collective-permute-start.57) | collective-permute-done | bytes 442400 | tf_op jit(solution)/shard_map/ppermute | solution.py:103
  469.2 12.1 %collective-permute-done.72 = bf16[192,1152]{1,0:T(8,128)(2,1)} collective-permute-done((bf16[192,1152]{1,0:T(8,128)(2,1)S(1)}, bf16[192,1152]{1,0:T(8,128)(2,1)}, u32[]{:S(2)}, u32[]{:S(2)}) %collective-permute-start.72) | collective-permute-done | bytes 442400 | tf_op jit(solution)/shard_map/ppermute | solution.py:103
  484.8 8.0 %collective-permute-done.58 = bf16[192,1152]{1,0:T(8,128)(2,1)} collective-permute-done((bf16[192,1152]{1,0:T(8,128)(2,1)S(1)}, bf16[192,1152]{1,0:T(8,128)(2,1)}, u32[]{:S(2)}, u32[]{:S(2)}) %collective-permute-start.58) | collective-permute-done | bytes 442400 | tf_op jit(solution)/shard_map/ppermute | solution.py:103
  499.2 10.0 %collective-permute-done.36 = bf16[48,1536]{1,0:T(8,128)(2,1)S(1)} collective-permute-done((bf16[48,1536]{1,0:T(8,128)(2,1)S(1)}, bf16[48,1536]{1,0:T(8,128)(2,1)S(1)}, u32[]{:S(2)}, u32[]{:S(2)}) %collective-permute-start.36) | collective-permute-done | bytes 147488 | tf_op jit(solution)/shard_map/ppermute | solution.py:90
  515.8 5.4 collective-permute-done.37
  541.3 9.1 %collective-permute-done.15 = f32[2,1536]{1,0:T(2,128)S(1)} collective-permute-done((f32[2,1536]{1,0:T(2,128)S(1)}, f32[2,1536]{1,0:T(2,128)S(1)}, u32[]{:S(2)}, u32[]{:S(2)}) %collective-permute-start.15) | collective-permute-done | bytes 12320 | tf_op jit(solution)/shard_map/ppermute | solution.py:119
  579.3 7.0 %collective-permute-done.42 = bf16[48,1536]{1,0:T(8,128)(2,1)S(1)} collective-permute-done((bf16[48,1536]{1,0:T(8,128)(2,1)S(1)}, bf16[48,1536]{1,0:T(8,128)(2,1)S(1)}, u32[]{:S(2)}, u32[]{:S(2)}) %collective-permute-start.42) | collective-permute-done | bytes 147488 | tf_op jit(solution)/shard_map/ppermute | solution.py:90
  640.3 11.2 %pad_maximum_fusion = f32[2,1536,1152]{2,1,0:T(8,128)} fusion(f32[1,1536,1152]{2,1,0:T(8,128)} %convert_dynamic-update-slice_fusion, f32[1,1536,1152]{2,1,0:T(8,128)} %convert_dynamic-update-slice_fusion.8), kind=kLoop, calls=%fused_computation.1 | loop fusion | flops 3538944 | bytes 28311552 | tf_op jit(solution)/shard_map/stack | solution.py:205
  661.1 9.6 %collective-permute-done.34 = bf16[1536,128]{1,0:T(8,128)(2,1)S(1)} collective-permute-done((bf16[1536,128]{1,0:T(8,128)(2,1)S(1)}, bf16[1536,128]{1,0:T(8,128)(2,1)S(1)}, u32[]{:S(2)}, u32[]{:S(2)}) %collective-permute-start.34) | collective-permute-done | bytes 393248 | tf_op jit(solution)/shard_map/ppermute | solution.py:57
  (505 shorter events, 367.9 us)
Async XLA Ops:
  1.2 49.2 %collective-permute-start.1 = (bf16[384,1536]{1,0:T(8,128)(2,1)}, bf16[384,1536]{1,0:T(8,128)(2,1)}, u32[]{:S(2)}, u32[]{:S(2)}) collective-permute-start(bf16[384,1536]{1,0:T(8,128)(2,1)} %param.15), channel_id=1, source_target_pairs={{0,1},{1,0},{2,3},{3,2},{4,5},{5,4},{6,7},{7,6},{8,9},{9,8},{10,11... | collective-permute-start | bytes 3538952 | tf_op jit(solution)/shard_map/ppermute | solution.py:53
  56.1 35.6 %collective-permute-start.2 = (bf16[480,1536]{1,0:T(8,128)(2,1)S(1)}, bf16[480,1536]{1,0:T(8,128)(2,1)S(1)}, u32[]{:S(2)}, u32[]{:S(2)}) collective-permute-start(bf16[480,1536]{1,0:T(8,128)(2,1)S(1)} %convolution_convert_fusion.4), channel_id=1, source_target_pairs={{0,2},{1,3},{2,0},{3,1},{4,6},{5,7},{6,4},{7,5},{8,10},{9,11},{10,... | collective-permute-start | bytes 4423688 | tf_op jit(solution)/shard_map/ppermute | solution.py:57
  96.9 33.5 %collective-permute-start.3 = (bf16[480,1536]{1,0:T(8,128)(2,1)}, bf16[480,1536]{1,0:T(8,128)(2,1)}, u32[]{:S(2)}, u32[]{:S(2)}) collective-permute-start(bf16[480,1536]{1,0:T(8,128)(2,1)} %get-tuple-element.32), channel_id=1, source_target_pairs={{0,1},{1,0},{2,3},{3,2},{4,5},{5,4},{6,7},{7,6},{8,9},{9,8},{10,11... | collective-permute-start | bytes 4423688 | tf_op jit(solution)/shard_map/ppermute | solution.py:53
  164.4 100.1 %collective-permute-start.4 = (bf16[480,1536]{1,0:T(8,128)(2,1)S(1)}, bf16[480,1536]{1,0:T(8,128)(2,1)S(1)}, u32[]{:S(2)}, u32[]{:S(2)}) collective-permute-start(bf16[480,1536]{1,0:T(8,128)(2,1)S(1)} %dynamic-slice_convert_fusion.1), channel_id=1, source_target_pairs={{0,1},{1,0},{2,3},{3,2},{4,5},{5,4},{6,7},{7,6},{8,9},{9,8},{10,11... | collective-permute-start | bytes 4423688 | tf_op jit(solution)/shard_map/ppermute | solution.py:53
  179.0 89.1 %collective-permute-start.7 = (bf16[480,1536]{1,0:T(8,128)(2,1)S(1)}, bf16[480,1536]{1,0:T(8,128)(2,1)S(1)}, u32[]{:S(2)}, u32[]{:S(2)}) collective-permute-start(bf16[480,1536]{1,0:T(8,128)(2,1)S(1)} %dynamic-slice_convert_fusion), channel_id=1, source_target_pairs={{0,1},{1,0},{2,3},{3,2},{4,5},{5,4},{6,7},{7,6},{8,9},{9,8},{10,11... | collective-permute-start | bytes 4423688 | tf_op jit(solution)/shard_map/ppermute | solution.py:53
  179.6 25.3 %collective-permute-start.64 = (bf16[192,1152]{1,0:T(8,128)(2,1)S(1)}, bf16[192,1152]{1,0:T(8,128)(2,1)S(1)}, u32[]{:S(2)}, u32[]{:S(2)}) collective-permute-start(bf16[192,1152]{1,0:T(8,128)(2,1)S(1)} %constant_dynamic-slice_fusion.2), channel_id=1, source_target_pairs={{4,12},{12,20},{20,28},{28,24},{24,16},{16,8},{8,0},{0,4},{5,13},{... | collective-permute-start | bytes 1327112 | tf_op jit(solution)/shard_map/ppermute | solution.py:90
  183.4 22.1 %collective-permute-start.50 = (bf16[192,1152]{1,0:T(8,128)(2,1)S(1)}, bf16[192,1152]{1,0:T(8,128)(2,1)S(1)}, u32[]{:S(2)}, u32[]{:S(2)}) collective-permute-start(bf16[192,1152]{1,0:T(8,128)(2,1)S(1)} %constant_dynamic-slice_fusion.3), channel_id=1, source_target_pairs={{0,8},{8,16},{16,24},{24,28},{28,20},{20,12},{12,4},{4,0},{1,9},{9... | collective-permute-start | bytes 1327112 | tf_op jit(solution)/shard_map/ppermute | solution.py:90
  205.6 25.1 %collective-permute-start.65 = (bf16[192,1152]{1,0:T(8,128)(2,1)S(1)}, bf16[192,1152]{1,0:T(8,128)(2,1)S(1)}, u32[]{:S(2)}, u32[]{:S(2)}) collective-permute-start(bf16[192,1152]{1,0:T(8,128)(2,1)S(1)} %add_convert_fusion.10), channel_id=1, source_target_pairs={{4,12},{12,20},{20,28},{28,24},{24,16},{16,8},{8,0},{0,4},{5,13},{... | collective-permute-start | bytes 1327112 | tf_op jit(solution)/shard_map/ppermute | solution.py:90
  231.6 23.4 %collective-permute-start.66 = (bf16[192,1152]{1,0:T(8,128)(2,1)S(1)}, bf16[192,1152]{1,0:T(8,128)(2,1)S(1)}, u32[]{:S(2)}, u32[]{:S(2)}) collective-permute-start(bf16[192,1152]{1,0:T(8,128)(2,1)S(1)} %add_convert_fusion.9), channel_id=1, source_target_pairs={{4,12},{12,20},{20,28},{28,24},{24,16},{16,8},{8,0},{0,4},{5,13},{... | collective-permute-start | bytes 1327112 | tf_op jit(solution)/shard_map/ppermute | solution.py:90
  256.3 22.6 %collective-permute-start.67 = (bf16[192,1152]{1,0:T(8,128)(2,1)S(1)}, bf16[192,1152]{1,0:T(8,128)(2,1)S(1)}, u32[]{:S(2)}, u32[]{:S(2)}) collective-permute-start(bf16[192,1152]{1,0:T(8,128)(2,1)S(1)} %add_convert_fusion.8), channel_id=1, source_target_pairs={{4,12},{12,20},{20,28},{28,24},{24,16},{16,8},{8,0},{0,4},{5,13},{... | collective-permute-start | bytes 1327112 | tf_op jit(solution)/shard_map/ppermute | solution.py:90
  268.2 119.9 %collective-permute-start.5 = (bf16[480,1536]{1,0:T(8,128)(2,1)}, bf16[480,1536]{1,0:T(8,128)(2,1)}, u32[]{:S(2)}, u32[]{:S(2)}) collective-permute-start(bf16[480,1536]{1,0:T(8,128)(2,1)} %add_convert_fusion.2), channel_id=1, source_target_pairs={{0,2},{1,3},{2,0},{3,1},{4,6},{5,7},{6,4},{7,5},{8,10},{9,11},{10,... | collective-permute-start | bytes 4423688 | tf_op jit(solution)/shard_map/ppermute | solution.py:57
  270.4 78.6 %collective-permute-start.8 = (bf16[480,1536]{1,0:T(8,128)(2,1)S(1)}, bf16[480,1536]{1,0:T(8,128)(2,1)S(1)}, u32[]{:S(2)}, u32[]{:S(2)}) collective-permute-start(bf16[480,1536]{1,0:T(8,128)(2,1)S(1)} %add_convert_fusion), channel_id=1, source_target_pairs={{0,2},{1,3},{2,0},{3,1},{4,6},{5,7},{6,4},{7,5},{8,10},{9,11},{10,... | collective-permute-start | bytes 4423688 | tf_op jit(solution)/shard_map/ppermute | solution.py:57
  301.5 22.1 %collective-permute-start.69 = (bf16[192,1152]{1,0:T(8,128)(2,1)S(1)}, bf16[192,1152]{1,0:T(8,128)(2,1)S(1)}, u32[]{:S(2)}, u32[]{:S(2)}) collective-permute-start(bf16[192,1152]{1,0:T(8,128)(2,1)S(1)} %add_convert_fusion.6), channel_id=1, source_target_pairs={{4,12},{12,20},{20,28},{28,24},{24,16},{16,8},{8,0},{0,4},{5,13},{... | collective-permute-start | bytes 1327112 | tf_op jit(solution)/shard_map/ppermute | solution.py:90
  326.0 81.3 %collective-permute-start.70 = (bf16[192,1152]{1,0:T(8,128)(2,1)}, bf16[192,1152]{1,0:T(8,128)(2,1)}, u32[]{:S(2)}, u32[]{:S(2)}) collective-permute-start(bf16[192,1152]{1,0:T(8,128)(2,1)} %add_convert_fusion.5), channel_id=1, source_target_pairs={{4,12},{12,20},{20,28},{28,24},{24,16},{16,8},{8,0},{0,4},{5,13},{... | collective-permute-start | bytes 1327112 | tf_op jit(solution)/shard_map/ppermute | solution.py:90
  330.5 82.6 %collective-permute-start.56 = (bf16[192,1152]{1,0:T(8,128)(2,1)}, bf16[192,1152]{1,0:T(8,128)(2,1)}, u32[]{:S(2)}, u32[]{:S(2)}) collective-permute-start(bf16[192,1152]{1,0:T(8,128)(2,1)} %add_convert_fusion.12), channel_id=1, source_target_pairs={{0,8},{8,16},{16,24},{24,28},{28,20},{20,12},{12,4},{4,0},{1,9},{9... | collective-permute-start | bytes 1327112 | tf_op jit(solution)/shard_map/ppermute | solution.py:90
  346.7 72.0 %collective-permute-start.105 = (bf16[144,768]{1,0:T(8,128)(2,1)}, bf16[144,768]{1,0:T(8,128)(2,1)}, u32[]{:S(2)}, u32[]{:S(2)}) collective-permute-start(bf16[144,768]{1,0:T(8,128)(2,1)} %collective-permute-done.104), channel_id=1, source_target_pairs={{4,12},{12,20},{20,28},{28,24},{24,16},{16,8},{8,0},{0,4},{5,13},{... | collective-permute-start | bytes 663560 | tf_op jit(solution)/shard_map/ppermute | solution.py:103
  349.0 72.0 %collective-permute-start.91 = (bf16[144,768]{1,0:T(8,128)(2,1)}, bf16[144,768]{1,0:T(8,128)(2,1)}, u32[]{:S(2)}, u32[]{:S(2)}) collective-permute-start(bf16[144,768]{1,0:T(8,128)(2,1)} %collective-permute-done.90), channel_id=1, source_target_pairs={{0,8},{8,16},{16,24},{24,28},{28,20},{20,12},{12,4},{4,0},{1,9},{9... | collective-permute-start | bytes 663560 | tf_op jit(solution)/shard_map/ppermute | solution.py:103
  391.9 138.3 %collective-permute-start.6 = (bf16[480,1536]{1,0:T(8,128)(2,1)}, bf16[480,1536]{1,0:T(8,128)(2,1)}, u32[]{:S(2)}, u32[]{:S(2)}) collective-permute-start(bf16[480,1536]{1,0:T(8,128)(2,1)} %get-tuple-element.30), channel_id=1, source_target_pairs={{0,1},{1,0},{2,3},{3,2},{4,5},{5,4},{6,7},{7,6},{8,9},{9,8},{10,11... | collective-permute-start | bytes 4423688 | tf_op jit(solution)/shard_map/ppermute | solution.py:53
  407.3 114.2 %collective-permute-start.9 = (bf16[480,1536]{1,0:T(8,128)(2,1)S(1)}, bf16[480,1536]{1,0:T(8,128)(2,1)S(1)}, u32[]{:S(2)}, u32[]{:S(2)}) collective-permute-start(bf16[480,1536]{1,0:T(8,128)(2,1)S(1)} %convolution_convert_fusion.3), channel_id=1, source_target_pairs={{0,2},{1,3},{2,0},{3,1},{4,6},{5,7},{6,4},{7,5},{8,10},{9,11},{10,... | collective-permute-start | bytes 4423688 | tf_op jit(solution)/shard_map/ppermute | solution.py:57
  418.7 78.5 %collective-permute-start.17 = (bf16[1536,384]{1,0:T(8,128)(2,1)S(1)}, bf16[1536,384]{1,0:T(8,128)(2,1)S(1)}, u32[]{:S(2)}, u32[]{:S(2)}) collective-permute-start(bf16[1536,384]{1,0:T(8,128)(2,1)S(1)} %slice.272), channel_id=1, source_target_pairs={{0,1},{1,0},{2,3},{3,2},{4,5},{5,4},{6,7},{7,6},{8,9},{9,8},{10,11... | collective-permute-start | bytes 3538952 | tf_op jit(solution)/shard_map/ppermute | solution.py:53
  420.9 74.4 %collective-permute-start.35 = (bf16[384,1536]{1,0:T(8,128)(2,1)S(1)}, bf16[384,1536]{1,0:T(8,128)(2,1)S(1)}, u32[]{:S(2)}, u32[]{:S(2)}) collective-permute-start(bf16[384,1536]{1,0:T(8,128)(2,1)S(1)} %slice.271), channel_id=1, source_target_pairs={{0,1},{1,0},{2,3},{3,2},{4,5},{5,4},{6,7},{7,6},{8,9},{9,8},{10,11... | collective-permute-start | bytes 3538952 | tf_op jit(solution)/shard_map/ppermute | solution.py:53
  422.8 23.6 %collective-permute-start.11 = (bf16[480,256]{1,0:T(8,128)(2,1)S(1)}, bf16[480,256]{1,0:T(8,128)(2,1)S(1)}, u32[]{:S(2)}, u32[]{:S(2)}) collective-permute-start(bf16[480,256]{1,0:T(8,128)(2,1)S(1)} %add_convert_fusion.19), channel_id=1, source_target_pairs={{0,2},{1,3},{2,0},{3,1},{4,6},{5,7},{6,4},{7,5},{8,10},{9,11},{10,... | collective-permute-start | bytes 737288 | tf_op jit(solution)/shard_map/ppermute | solution.py:57
  492.8 41.1 %collective-permute-start.73 = (bf16[192,1152]{1,0:T(8,128)(2,1)}, bf16[192,1152]{1,0:T(8,128)(2,1)}, u32[]{:S(2)}, u32[]{:S(2)}) collective-permute-start(bf16[192,1152]{1,0:T(8,128)(2,1)} %collective-permute-done.72), channel_id=1, source_target_pairs={{4,12},{12,20},{20,28},{28,24},{24,16},{16,8},{8,0},{0,4},{5,13},{... | collective-permute-start | bytes 1327112 | tf_op jit(solution)/shard_map/ppermute | solution.py:103
  495.3 43.1 %collective-permute-start.59 = (bf16[192,1152]{1,0:T(8,128)(2,1)}, bf16[192,1152]{1,0:T(8,128)(2,1)S(1)}, u32[]{:S(2)}, u32[]{:S(2)}) collective-permute-start(bf16[192,1152]{1,0:T(8,128)(2,1)} %collective-permute-done.58), channel_id=1, source_target_pairs={{0,8},{8,16},{16,24},{24,28},{28,20},{20,12},{12,4},{4,0},{1,9},{9... | collective-permute-start | bytes 1327112 | tf_op jit(solution)/shard_map/ppermute | solution.py:103
  521.2 30.2 %collective-permute-start.20 = (bf16[224,384]{1,0:T(8,128)(2,1)S(1)}, bf16[224,384]{1,0:T(8,128)(2,1)S(1)}, u32[]{:S(2)}, u32[]{:S(2)}) collective-permute-start(bf16[224,384]{1,0:T(8,128)(2,1)S(1)} %add_convert_fusion.42), channel_id=1, source_target_pairs={{4,12},{12,20},{20,28},{28,24},{24,16},{16,8},{8,0},{0,4},{5,13},{... | collective-permute-start | bytes 516104 | tf_op jit(solution)/shard_map/ppermute | solution.py:90
  521.5 32.8 %collective-permute-start.38 = (bf16[48,1536]{1,0:T(8,128)(2,1)S(1)}, bf16[48,1536]{1,0:T(8,128)(2,1)S(1)}, u32[]{:S(2)}, u32[]{:S(2)}) collective-permute-start(bf16[48,1536]{1,0:T(8,128)(2,1)S(1)} %add_convert_fusion.48), channel_id=1, source_target_pairs={{0,8},{8,16},{16,24},{24,28},{28,20},{20,12},{12,4},{4,0},{1,9},{9... | collective-permute-start | bytes 442376 | tf_op jit(solution)/shard_map/ppermute | solution.py:90
  533.9 89.8 %collective-permute-start.12 = (bf16[480,1536]{1,0:T(8,128)(2,1)S(1)}, bf16[480,1536]{1,0:T(8,128)(2,1)S(1)}, u32[]{:S(2)}, u32[]{:S(2)}) collective-permute-start(bf16[480,1536]{1,0:T(8,128)(2,1)S(1)} %get-tuple-element.26), channel_id=1, source_target_pairs={{0,1},{1,0},{2,3},{3,2},{4,5},{5,4},{6,7},{7,6},{8,9},{9,8},{10,11... | collective-permute-start | bytes 4423688 | tf_op jit(solution)/shard_map/ppermute | solution.py:53
  537.7 33.8 %collective-permute-start.74 = (bf16[192,1152]{1,0:T(8,128)(2,1)}, bf16[192,1152]{1,0:T(8,128)(2,1)S(1)}, u32[]{:S(2)}, u32[]{:S(2)}) collective-permute-start(bf16[192,1152]{1,0:T(8,128)(2,1)} %collective-permute-done.73), channel_id=1, source_target_pairs={{4,12},{12,20},{20,28},{28,24},{24,16},{16,8},{8,0},{0,4},{5,13},{... | collective-permute-start | bytes 1327112 | tf_op jit(solution)/shard_map/ppermute | solution.py:103
  571.4 23.2 %collective-permute-start.75 = (bf16[192,1152]{1,0:T(8,128)(2,1)S(1)}, bf16[192,1152]{1,0:T(8,128)(2,1)S(1)}, u32[]{:S(2)}, u32[]{:S(2)}) collective-permute-start(bf16[192,1152]{1,0:T(8,128)(2,1)S(1)} %collective-permute-done.74), channel_id=1, source_target_pairs={{4,12},{12,20},{20,28},{28,24},{24,16},{16,8},{8,0},{0,4},{5,13},{... | collective-permute-start | bytes 1327112 | tf_op jit(solution)/shard_map/ppermute | solution.py:103
  572.4 23.3 %collective-permute-start.61 = (bf16[192,1152]{1,0:T(8,128)(2,1)S(1)}, bf16[192,1152]{1,0:T(8,128)(2,1)S(1)}, u32[]{:S(2)}, u32[]{:S(2)}) collective-permute-start(bf16[192,1152]{1,0:T(8,128)(2,1)S(1)} %collective-permute-done.60), channel_id=1, source_target_pairs={{0,8},{8,16},{16,24},{24,28},{28,20},{20,12},{12,4},{4,0},{1,9},{9... | collective-permute-start | bytes 1327112 | tf_op jit(solution)/shard_map/ppermute | solution.py:103
  594.7 22.1 %collective-permute-start.76 = (bf16[192,1152]{1,0:T(8,128)(2,1)S(1)}, bf16[192,1152]{1,0:T(8,128)(2,1)S(1)}, u32[]{:S(2)}, u32[]{:S(2)}) collective-permute-start(bf16[192,1152]{1,0:T(8,128)(2,1)S(1)} %collective-permute-done.75), channel_id=1, source_target_pairs={{4,12},{12,20},{20,28},{28,24},{24,16},{16,8},{8,0},{0,4},{5,13},{... | collective-permute-start | bytes 1327112 | tf_op jit(solution)/shard_map/ppermute | solution.py:103
  595.7 22.1 %collective-permute-start.62 = (bf16[192,1152]{1,0:T(8,128)(2,1)S(1)}, bf16[192,1152]{1,0:T(8,128)(2,1)S(1)}, u32[]{:S(2)}, u32[]{:S(2)}) collective-permute-start(bf16[192,1152]{1,0:T(8,128)(2,1)S(1)} %collective-permute-done.61), channel_id=1, source_target_pairs={{0,8},{8,16},{16,24},{24,28},{28,20},{20,12},{12,4},{4,0},{1,9},{9... | collective-permute-start | bytes 1327112 | tf_op jit(solution)/shard_map/ppermute | solution.py:103
  (130 other events, 1602.6 us)

commit v2 on v0

v2 whole, which is shorter than its diff:
```python
import functools
import math

import jax
import jax.numpy as jnp
import numpy as np
from jax import lax
from jax.experimental import pallas as pl
from jax.experimental.pallas import tpu as pltpu
from jax.sharding import PartitionSpec as P

WINDOW = 1024
EPSILON = 1e-06
GELU_COEF = 0.7978845608028654
BF16 = jnp.bfloat16
F32 = jnp.float32
NN = (((1,), (0,)), ((), ()))
NT = (((1,), (1,)), ((), ()))
TN = (((0,), (0,)), ((), ()))

RING = (0, 2, 4, 6, 7, 5, 3, 1)

ANY = pl.BlockSpec(memory_space=pl.ANY)
SMEM = pl.BlockSpec(memory_space=pltpu.SMEM)
MIB = 2**20

ORDER = " ".join(
    (
        "project attend0 attend1 dhidden",
        "norm0 ffn0 norm1 ffn1",
        "down gate a up",
        "a dnsib a b",
        "dnown a b a",
        "a b a nback",
        "aback a b qg",
        "a kv b a",
        "kvpart outg a b",
        "dn1 a b a",
        "a b E fosib",
        "a b a foown",
        "a b a a",
        "b a input sums",
        "a b a out",
        "weave a b a",
        "a b a a",
        "a",
    )
).split()


def dot(left, right, dims=NN):
    return lax.dot_general(left, right, dims, preferred_element_type=F32)


def swap_core(field):
    return lax.ppermute(field, "tensor", [(i, i ^ 1) for i in range(4)])


def swap_x(field):
    return lax.ppermute(field, "tensor", [(i, i ^ 2) for i in range(4)])


def shape(dims, dtype):
    return jax.ShapeDtypeStruct(dims, dtype)


def whole(array):
    rank = len(array.shape)
    return pl.BlockSpec(array.shape, lambda *_: (0,) * rank)


class Chain:
    def __init__(self):
        self.links = []

    def call(self, body, outs, ins, in_specs, out_specs, grid=(), scalars=(), vmem=24, scratch=(), aliases=None):
        links, given = self.links, len(scalars) + len(ins)

        def run(*refs):
            body(*refs[:given], *refs[given + len(links) :])

        results = pl.pallas_call(
            run,
            out_shape=outs,
            grid_spec=pltpu.PrefetchScalarGridSpec(
                num_scalar_prefetch=len(scalars),
                grid=grid,
                in_specs=list(in_specs) + [ANY] * len(links),
                out_specs=out_specs,
                scratch_shapes=list(scratch),
            ),
            input_output_aliases=aliases or {},
            compiler_params=pltpu.CompilerParams(vmem_limit_bytes=vmem * MIB),
            cost_estimate=pl.CostEstimate(flops=0, bytes_accessed=0, transcendentals=0),
        )(*scalars, *ins, *links)
        self.links = [results[0]]
        return results

    def after(self, *values):
        tied = lax.optimization_barrier(values + tuple(self.links))
        self.links = list(tied[len(values) :])
        return tied[: len(values)]


def rope(field, table, sign=1.0):
    half = field.shape[1] // 2
    other = pltpu.roll(table, half, 1)
    first = lax.broadcasted_iota(jnp.int32, table.shape, 1) < half
    cosine = jnp.where(first, table, other)
    sine = jnp.where(first, -other, table) * sign
    return field * cosine + pltpu.roll(field, half, 1) * sine


def rms_factor(field):
    return lax.rsqrt(jnp.mean(field * field, axis=1, keepdims=True) + EPSILON)


def project_kernel(core, x, gain, weight, table, keys, values, own0, own1):
    block = pl.program_id(0)
    head_dim = keys.shape[1]
    field = x[...].astype(F32)
    normed = (field * rms_factor(field) * gain[...]).astype(BF16)
    both = dot(normed, weight[...])
    keys[...] = rope(both[:, :head_dim], table[...]).astype(BF16)
    values[...] = both[:, head_dim:].astype(BF16)

    @pl.when(core[0] == block)
    def _():
        own0[...] = normed

    @pl.when(3 - core[0] == block)
    def _():
        own1[...] = normed


def causal(rows, columns, first_row):
    row = lax.broadcasted_iota(jnp.int32, (rows, columns), 0) + first_row
    column = lax.broadcasted_iota(jnp.int32, (rows, columns), 1)
    allowed = column <= row
    if columns > WINDOW:
        allowed = allowed & (row - column < WINDOW)
    return allowed


def attend_kernel(
    numbers, scale, block, normed, keys, values, table, query_own, query_sib, out_own, out_sib,
    part, rot_q, head_out, log_total, query_w, out_w, arrived,
):
    quarter = normed.shape[0]
    head_dim = keys.shape[1]
    per_core = query_own.shape[1] // head_dim
    copies = [
        pltpu.make_async_copy(source, target, arrived.at[i])
        for i, (source, target) in enumerate(
            ((query_own, query_w.at[0]), (query_sib, query_w.at[1]), (out_own, out_w.at[0]), (out_sib, out_w.at[1]))
        )
    ]
    for copy in copies:
        copy.start()
    for side in range(2):
        copies[side].wait()
        queries = dot(normed[...], query_w[side])
        for head in range(per_core):
            columns = slice(head * head_dim, (head + 1) * head_dim)
            place = side * per_core + head
            rot_q[:, place * head_dim : (place + 1) * head_dim] = (
                rope(queries[:, columns], table[...]) * scale
            ).astype(BF16)
    for number in numbers:

        @pl.when(block[0] == number)
        def _():
            span = (number + 1) * quarter
            allowed = causal(quarter, span, number * quarter)
            for head in range(2 * per_core):
                columns = slice(head * head_dim, (head + 1) * head_dim)
                scores = dot(rot_q[:, columns], keys[:span, :], NT)
                scores = jnp.where(allowed, scores, -1e30)
                top = jnp.max(scores, axis=1, keepdims=True)
                weights = jnp.exp(scores - top)
                total = jnp.sum(weights, axis=1, keepdims=True)
                probs = (weights * (1.0 / total)).astype(BF16)
                head_out[:, columns] = dot(probs, values[:span, :]).astype(BF16)
                log_total[:, head : head + 1] = top + jnp.log(total)

    copies[2].wait()
    copies[3].wait()
    half = per_core * head_dim
    part[...] = (dot(head_out[:, :half], out_w[0]) + dot(head_out[:, half:], out_w[1])).astype(BF16)


def attend_back_kernel(
    scale, core, rot_q0, rot_q1, log0, log1, d_heads, keys, values, table,
    d_queries, kv_own, kv_sib, d_keys, d_values,
):
    quarter = rot_q0.shape[0]
    head_dim = keys.shape[1]
    heads = rot_q0.shape[1] // head_dim
    d_keys[...] = jnp.zeros_like(d_keys)
    d_values[...] = jnp.zeros_like(d_values)

    def rows_of(block):
        return pl.ds(pl.multiple_of(block * quarter, 16), quarter)

    for order, (rot_q, log_total) in enumerate(((rot_q0, log0), (rot_q1, log1))):
        block = core[0] if order == 0 else 3 - core[0]
        rows = slice(order * quarter, (order + 1) * quarter)
        for number in (0, 1) if order == 0 else (2, 3):

            @pl.when(block == number)
            def _():
                span = (number + 1) * quarter
                own_table = table[number * quarter : span, :]
                allowed = causal(quarter, span, number * quarter)
                for head in range(heads):
                    columns = slice(head * head_dim, (head + 1) * head_dim)
                    query = rot_q[:, columns]
                    d_out = d_heads[rows, columns]
                    scores = dot(query, keys[:span, :], NT) - log_total[:, head : head + 1]
                    probs = jnp.exp(jnp.where(allowed, scores, -1e30))
                    d_probs = dot(d_out, values[:span, :], NT)
                    delta = jnp.sum(probs * d_probs, axis=1, keepdims=True)
                    d_scores = (probs * (d_probs - delta)).astype(BF16)
                    d_query = dot(d_scores, keys[:span, :]) * scale
                    d_queries[rows, columns] = rope(d_query, own_table, -1.0).astype(BF16)
                    d_keys[:span, :] += dot(d_scores, query, TN)
                    d_values[:span, :] += dot(probs.astype(BF16), d_out, TN)

    d_keys[...] = rope(d_keys[...], table[...], -1.0)
    for order in range(2):
        rows = slice(order * quarter, (order + 1) * quarter)
        own = rows_of(core[0] if order == 0 else 3 - core[0])
        sib = rows_of(1 - core[0] if order == 0 else 2 + core[0])
        kv_own[rows, :head_dim] = d_keys[own, :]
        kv_own[rows, head_dim:] = d_values[own, :]
        kv_sib[rows, :head_dim] = d_keys[sib, :].astype(BF16)
        kv_sib[rows, head_dim:] = d_values[sib, :].astype(BF16)


def d_hidden_kernel(places, cotangent, weight, d_hidden, ordered):
    d_hidden[...] = dot(cotangent[...], weight[...], NT).astype(BF16)
    ordered[...] = cotangent[...]


def norm_kernel(block, x, part, from_x, gain, *rest):
    normed, residual = rest[-2:]
    value = x[...].astype(F32) + (part[...].astype(F32) + from_x[...].astype(F32))
    residual[...] = value
    normed[...] = (value * rms_factor(value) * gain[...]).astype(BF16)


def ffn_kernel(normed_own, normed_sib, weight, d_hidden, *rest):
    hidden, d_gate, d_up, normed_all = rest[-4:]
    quarter = normed_own.shape[0]

    @pl.when(pl.program_id(0) == 0)
    def _():
        normed_all[:quarter, :] = normed_own[...]
        normed_all[quarter:, :] = normed_sib[...]

    gate = dot(normed_all[...], weight[0])
    up = dot(normed_all[...], weight[1])
    square = gate * gate
    inner = jnp.tanh(GELU_COEF * gate * (1.0 + 0.044715 * square))
    half = 0.5 * (1.0 + inner)
    gelu = gate * half
    slope = half + 0.5 * gate * (1.0 - inner * inner) * (GELU_COEF * (1.0 + 3.0 * 0.044715 * square))
    back = d_hidden[...].astype(F32)
    hidden[...] = (gelu * up).astype(BF16)
    d_gate[...] = (back * up * slope).astype(BF16)
    d_up[...] = (back * gelu).astype(BF16)


def grad_kernel(left, right, out):
    out[...] = dot(left[...], right[...], TN).astype(BF16)


def rows_back_kernel(dims, count, *refs):
    lefts, rights, rest = refs[:count], refs[count : 2 * count], refs[2 * count :]
    out = rest[-1]
    total = None
    for left, right in zip(lefts, rights):
        rows = left[...].reshape(-1, left.shape[-1])
        matrix = right[...]
        term = dot(rows, matrix.reshape(matrix.shape[-2:]), dims)
        total = term if total is None else total + term
    if len(rest) == 2:
        total = total + rest[0][...].astype(F32)
    out[...] = total.astype(BF16)


def norm_back(field, gain, d_normed):
    factor = rms_factor(field)
    scaled = gain * d_normed
    d_gain = jnp.sum(d_normed * field * factor, axis=0, keepdims=True)
    return factor * scaled - field * (factor * factor * factor) * jnp.mean(scaled * field, axis=1, keepdims=True), d_gain


def norm2_back_kernel(
    residual, on_chip, from_x, cotangent, gain, out_own, out_sib, d_residual, d_res_low, d_heads, d_gain
):
    d_normed = on_chip[...].astype(F32) + from_x[...].astype(F32)
    change, part = norm_back(residual[...], gain[...], d_normed)
    total = cotangent[...].reshape(residual.shape).astype(F32) + change
    d_residual[...] = total
    low = total.astype(BF16)
    d_res_low[...] = low
    half = out_own.shape[0]
    d_heads[:, :half] = dot(low, out_own[...], NT).astype(BF16)
    d_heads[:, half:] = dot(low, out_sib[...], NT).astype(BF16)

    @pl.when(pl.program_id(0) == 0)
    def _():
        d_gain[...] = part

    @pl.when(pl.program_id(0) > 0)
    def _():
        d_gain[...] += part


def norm1_back_kernel(places, x, on_chip, from_x, d_kv, kv_weight, d_residual, gain, d_input, d_gain):
    d_normed = (on_chip[...].astype(F32) + from_x[...].astype(F32)) + dot(d_kv[...], kv_weight[...], NT)
    change, part = norm_back(x[...].astype(F32), gain[...], d_normed)
    d_input[...] = (d_residual[...] + change).astype(BF16)

    @pl.when(pl.program_id(0) == 0)
    def _():
        d_gain[...] = part

    @pl.when(pl.program_id(0) > 0)
    def _():
        d_gain[...] += part


def split_grad_kernel(columns, left0, left1, right, mine, other):
    quarter = left0.shape[0]
    top, bottom = right[:quarter, :], right[quarter:, :]
    mine[...] = dot(left0[:, :columns], top, TN) + dot(left1[:, :columns], bottom, TN)
    other[...] = (dot(left0[:, columns:], top, TN) + dot(left1[:, columns:], bottom, TN)).astype(BF16)


def query_grad_kernel(columns, left0, left1, right, mine, other):
    quarter = left0.shape[0]
    mine[...] = dot(left0[...], right[:quarter, :columns], TN) + dot(left1[...], right[quarter:, :columns], TN)
    other[...] = (
        dot(left0[...], right[:quarter, columns:], TN) + dot(left1[...], right[quarter:, columns:], TN)
    ).astype(BF16)


def weave_kernel(places, own, sibling, out):
    step = pl.program_id(0)

    @pl.when(step < 2)
    def _():
        out[...] = own[...]

    @pl.when(step >= 2)
    def _():
        out[...] = sibling[...]


def empty(dims, dtype):
    return pl.pallas_call(lambda out: None, out_shape=shape(dims, dtype), out_specs=ANY)()


class Flow:
    def __init__(self, forward, chain):
        order = RING if forward else RING[::-1]
        self.chain = chain
        self.perm = [(order[i], order[(i + 1) % 8]) for i in range(8)]
        place = np.zeros(8, np.int32)
        for i, device in enumerate(order):
            place[device] = i
        place = jnp.asarray(place)[lax.axis_index("dp")]
        self.numbers = [(place - i) & 7 for i in range(8)]

    def chunk(self, i):
        parts = [
            lax.dynamic_slice(f, (self.numbers[i % 8], 0, 0), (1,) + f.shape[1:], allow_negative_indices=False)[0]
            for f in self.fields
        ]
        return parts[0] if len(parts) == 1 else jnp.concatenate(parts, 0)

    def begin(self, fields, write):
        self.fields, self.write, self.step = fields, write, 0
        self.travelling = self.chunk(1)
        self.arrived = lax.ppermute(self.travelling, "dp", self.perm)

    def land(self):
        step = self.step
        self.step += 1
        if step < 7:
            mine = self.chunk(step + 2)
            self.travelling = (self.arrived.astype(F32) + mine.astype(F32)).astype(BF16)
        else:
            self.travelling = self.arrived

    def send(self):
        if self.step < 14:
            self.arrived = lax.ppermute(self.travelling, "dp", self.perm)
        if self.step >= 7:
            self.write(self.numbers[(self.step - 7) % 8], self.travelling)


class Pair:
    def __init__(self, chain):
        self.chain = chain
        self.flows = (Flow(True, chain), Flow(False, chain))
        self.left = 0

    def begin(self, way, *job):
        self.flows[way].begin(*job)
        self.left = 14

    def step(self):
        if self.left == 0:
            raise ValueError("ring idle")
        self.left -= 1
        arrived = self.chain.after(*[flow.arrived for flow in self.flows])
        for flow, value in zip(self.flows, arrived):
            flow.arrived = value
            flow.land()
        self.chain.links = self.chain.links[:1] + [flow.travelling for flow in self.flows]
        for flow in self.flows:
            flow.send()


class Whole:
    left = 0

    def __init__(self, chain):
        pass

    def begin(self, way, fields, write):
        sums = [lax.psum(f, "dp") for f in fields]
        for k in range(8):
            write(k, jnp.concatenate([s[k] for s in sums], 0))

    def step(self):
        pass


def small_sum(field, n_dp):
    if n_dp & (n_dp - 1):
        field = lax.psum(field, "dp")
    else:
        step = 1
        while step < n_dp:
            field = field + lax.ppermute(field, "dp", [(i, i ^ step) for i in range(n_dp)])
            step *= 2
    return field + swap_core(field)


class Block:
    def __init__(self, n_dp, args):
        (
            self.x, self.gain1, self.query_w, self.kv_w, self.out_w, self.gain2, self.gate_up_w, self.down_w, self.cot_in,
        ) = args
        self.gain1, self.gain2 = self.gain1[None], self.gain2[None]
        self.n_dp = n_dp
        self.length, self.width = self.x.shape
        self.quarter, self.half = self.length // 4, self.length // 2
        self.head_dim = self.kv_w.shape[1] // 2
        self.cols = self.query_w.shape[1]
        self.units = self.down_w.shape[0]
        self.middle = self.width // 2
        self.scale = 1.0 / math.sqrt(self.head_dim)
        tensor = lax.axis_index("tensor")
        self.core, self.chip = tensor & 1, tensor >> 1
        core = self.core
        self.own = jnp.stack([core, 3 - core])
        self.places = jnp.stack([core, 1 - core, 3 - core, 2 + core])
        self.weave_places = jnp.stack([core, 3 - core, 1 - core, 2 + core])
        self.chain = Chain()
        ring = Pair if n_dp == 8 else Whole
        self.ring_a, self.ring_b = ring(self.chain), ring(self.chain)
        half_dim = self.head_dim // 2
        angle = np.arange(self.length)[:, None] * 10000.0 ** (-2.0 * np.arange(half_dim)[None, :] / self.head_dim)
        self.table = jnp.asarray(np.concatenate([np.cos(angle), np.sin(angle)], 1), F32)
        self.query_sib = swap_core(self.query_w)
        self.out_sib = swap_core(self.out_w)
        self.down_sum = empty((8, self.units // 8, self.width), F32)
        self.gate_up_sum = empty((2, 8, self.width // 8, self.units), F32)
        self.out_sum = empty((8, self.cols // 8, self.width), F32)
        self.query_sum = empty((8, self.width // 8, self.cols), F32)

    def rows(self, table=None):
        if table is None:
            return pl.BlockSpec((self.quarter, self.width), lambda i, *_: (i, 0))
        return pl.BlockSpec((self.quarter, self.width), lambda i, places: (places[i], 0))

    def project(self):
        q, d, w = self.quarter, self.head_dim, self.width
        same = pl.BlockSpec((q, w), lambda i, _: (0, 0))
        narrow = pl.BlockSpec((q, d), lambda i, _: (i, 0))
        self.keys, self.values, own0, own1 = self.chain.call(
            project_kernel,
            [shape((4 * q, d), BF16)] * 2 + [shape((q, w), BF16)] * 2,
            [self.x, self.gain1, self.kv_w, self.table],
            [pl.BlockSpec((q, w), lambda i, _: (i, 0)), whole(self.gain1), whole(self.kv_w), narrow],
            [narrow, narrow, same, same],
            grid=(4,),
            scalars=[self.core[None]],
        )
        self.normed1 = (own0, own1)

    def attend(self, j):
        q, w, c = self.quarter, self.width, 2 * self.cols
        normed = self.normed1[j]
        table = pl.BlockSpec((q, self.head_dim), lambda i, block: (block[0], 0))
        return self.chain.call(
            functools.partial(attend_kernel, (0, 1) if j == 0 else (2, 3), self.scale),
            [shape((q, w), BF16), shape((q, c), BF16), shape((q, c), BF16), shape((q, 8), F32)],
            [normed, self.keys, self.values, self.table, self.query_w, self.query_sib, self.out_w, self.out_sib],
            [whole(normed), whole(self.keys), whole(self.values), table] + [ANY] * 4,
            [pl.BlockSpec(d, lambda *_: (0, 0)) for d in ((q, w), (q, c), (q, c), (q, 8))],
            grid=(1,),
            scalars=[self.own[j][None]],
            scratch=[
                pltpu.VMEM((2,) + self.query_w.shape, BF16),
                pltpu.VMEM((2,) + self.out_w.shape, BF16),
                pltpu.SemaphoreType.DMA((4,)),
            ],
        )

    def attend0(self):
        self.part0, self.rot_q0, self.head_out0, self.log0 = self.attend(0)
        self.from_x0 = swap_x(self.part0)

    def attend1(self):
        self.part1, self.rot_q1, self.head_out1, self.log1 = self.attend(1)
        self.from_x1 = swap_x(self.part1)

    def dhidden(self):
        self.d_hidden, self.cot = self.chain.call(
            d_hidden_kernel,
            [shape((self.length, self.units), BF16), shape((self.length, self.width), BF16)],
            [self.cot_in, self.down_w],
            [self.rows(1), whole(self.down_w)],
            [pl.BlockSpec((self.quarter, self.units), lambda i, _: (i, 0)), self.rows()],
            grid=(4,),
            scalars=[self.places],
        )

    def norm(self, j, part, from_x, before):
        block = pl.BlockSpec((self.quarter, self.width), lambda i, _: (0, 0))
        return self.chain.call(
            norm_kernel,
            [shape((self.quarter, self.width), BF16), shape((self.half, self.width), F32)],
            [self.x, part, from_x, self.gain2, *before],
            [self.rows(1), block, block, whole(self.gain2)] + [ANY] * len(before),
            [block, pl.BlockSpec((self.quarter, self.width), lambda i, _: (j, 0))],
            grid=(1,),
            scalars=[self.own[j][None]],
            aliases={5: 1} if before else None,
        )

    def norm0(self):
        self.normed2_0, self.residual = self.norm(0, self.part0, self.from_x0, ())
        self.sib2_0 = swap_core(self.normed2_0)

    def norm1(self):
        self.normed2_1, self.residual = self.norm(1, self.part1, self.from_x1, (self.residual,))
        self.sib2_1 = swap_core(self.normed2_1)

    def ffn(self, j, own, sibling, before):
        tile = self.units // 3
        here = pl.BlockSpec((self.half, tile), lambda i: (j, i))
        return self.chain.call(
            ffn_kernel,
            [shape((self.length, self.units), BF16)] * 3 + [shape((self.length, self.width), BF16)],
            [own, sibling, self.gate_up_w, self.d_hidden, *before],
            [whole(own), whole(sibling), pl.BlockSpec((2, self.width, tile), lambda i: (0, 0, i)), here]
            + [ANY] * len(before),
            [here] * 3 + [pl.BlockSpec((self.half, self.width), lambda i: (j, 0))],
            grid=(3,),
            aliases={4 + i: i for i in range(len(before))},
            vmem=32,
        )

    def ffn0(self):
        self.wide = self.ffn(0, self.normed2_0, self.sib2_0, ())

    def ffn1(self):
        self.hidden, self.d_gate, self.d_up, self.normed2 = self.ffn(1, self.normed2_1, self.sib2_1, self.wide)

    def grad(self, left, right, tiles, column=0, columns=None):
        columns = columns or right.shape[1]
        tile = left.shape[1] // tiles
        return self.chain.call(
            grad_kernel,
            [shape((left.shape[1], columns), BF16)],
            [left, right],
            [
                pl.BlockSpec((self.length, tile), lambda i: (0, i)),
                pl.BlockSpec((self.length, columns), lambda i: (0, column)),
            ],
            [pl.BlockSpec((tile, columns), lambda i: (i, 0))],
            grid=(tiles,),
            vmem=28,
        )[0]

    def eight(self, field):
        return field.reshape(8, field.shape[0] // 8, field.shape[1])

    def down(self):
        for way in range(2):
            grad = self.grad(self.hidden, self.cot, 3, way, self.middle)

            def write(k, piece, way=way):
                self.down_sum = self.place(self.down_sum, piece[None], (k, 0, way * self.middle))

            self.ring_a.begin(way, [self.eight(grad)], write)

    @staticmethod
    def place(target, piece, position):
        return lax.dynamic_update_slice(target, piece.astype(F32), position, allow_negative_indices=False)

    def gate_up(self, way, d_wide):
        grad = self.grad(self.normed2, d_wide, 3)

        def write(k, piece):
            self.gate_up_sum = self.place(self.gate_up_sum, piece[None, None], (way, k, 0, 0))

        self.ring_b.begin(way, [self.eight(grad)], write)

    def gate(self):
        self.gate_up(0, self.d_gate)

    def up(self):
        self.gate_up(1, self.d_up)

    def rows_back(self, side, lefts, rights, specs, dims, extra=()):
        tile = self.width // 4
        lefts = [left.reshape(2, 2, self.quarter, self.units) for left in lefts]
        column = pl.BlockSpec((self.half, tile), lambda i: (0, i))
        return self.chain.call(
            functools.partial(rows_back_kernel, dims, len(lefts)),
            [shape((self.half, self.width), BF16)],
            [*lefts, *rights, *extra],
            [pl.BlockSpec((2, 1, self.quarter, self.units), lambda i: (0, side, 0, 0))] * len(lefts)
            + specs
            + [column] * len(extra),
            [column],
            grid=(4,),
        )[0]

    def dn(self, side, extra=()):
        tile = self.width // 4
        specs = [pl.BlockSpec((1, tile, self.units), lambda i, n=n: (n, i, 0)) for n in range(2)]
        return self.rows_back(side, [self.d_gate, self.d_up], [self.gate_up_w] * 2, specs, NT, extra)

    def dnsib(self):
        self.dn_from = swap_core(self.dn(1))

    def dnown(self):
        self.dn_chip = self.dn(0, (self.dn_from,))
        self.dn_x = swap_x(self.dn_chip)

    def fo(self, side, extra=()):
        tile = self.width // 4
        specs = [pl.BlockSpec((self.units, tile), lambda i: (0, i))]
        return self.rows_back(side, [self.hidden], [self.down_w], specs, NN, extra)

    def fosib(self):
        self.fo_from = swap_core(self.fo(1))

    def foown(self):
        self.fo_chip = self.fo(0, (self.fo_from,))
        self.fo_x = swap_x(self.fo_chip)

    def nback(self):
        q, w, c = self.quarter, self.width, 2 * self.cols
        self.d_residual, self.d_res_low, self.d_heads, self.norm2_part = self.chain.call(
            norm2_back_kernel,
            [shape((self.half, w), F32), shape((self.half, w), BF16), shape((self.half, c), BF16), shape((1, w), F32)],
            [
                self.residual, self.dn_chip, self.dn_x, self.cot.reshape(2, 2, q, w), self.gain2, self.out_w, self.out_sib,
            ],
            [
                self.rows(), self.rows(), self.rows(), pl.BlockSpec((1, 1, q, w), lambda i: (i, 0, 0, 0)),
                whole(self.gain2), whole(self.out_w), whole(self.out_sib),
            ],
            [self.rows(), self.rows(), pl.BlockSpec((q, c), lambda i: (i, 0)), pl.BlockSpec((1, w), lambda i: (0, 0))],
            grid=(2,),
            vmem=32,
        )

    def aback(self):
        ins = [self.rot_q0, self.rot_q1, self.log0, self.log1, self.d_heads, self.keys, self.values, self.table]
        outs = [
            shape((self.half, 2 * self.cols), BF16),
            shape((self.half, 2 * self.head_dim), F32),
            shape((self.half, 2 * self.head_dim), BF16),
        ]
        self.d_queries, self.kv_own, kv_sib = self.chain.call(
            functools.partial(attend_back_kernel, self.scale),
            outs,
            ins,
            [whole(a) for a in ins],
            [whole(a) for a in outs],
            grid=(1,),
            scalars=[self.core[None]],
            scratch=[pltpu.VMEM((self.length, self.head_dim), F32)] * 2,
        )
        self.kv_from = swap_core(kv_sib)

    def outg(self):
        outs = [shape(self.out_w.shape, F32), shape(self.out_w.shape, BF16)]
        ins = [self.head_out0, self.head_out1, self.d_res_low]
        self.out_mine, other = self.chain.call(
            functools.partial(split_grad_kernel, self.cols),
            outs, ins, [whole(a) for a in ins], [whole(a) for a in outs], grid=(1,),
        )
        self.out_from = swap_core(other)

    def qg(self):
        outs = [shape(self.query_w.shape, F32), shape(self.query_w.shape, BF16)]
        ins = [*self.normed1, self.d_queries]
        self.query_mine, other = self.chain.call(
            functools.partial(query_grad_kernel, self.cols),
            outs, ins, [whole(a) for a in ins], [whole(a) for a in outs], grid=(1,),
        )
        self.query_from = swap_core(other)

    def dn1(self):
        tile = self.width // 4
        row = pl.BlockSpec((tile, self.cols), lambda i: (i, 0))
        (self.dn1_chip,) = self.chain.call(
            functools.partial(rows_back_kernel, NT, 2),
            [shape((self.half, self.width), BF16)],
            [self.d_queries, self.d_queries, self.query_w, self.query_sib],
            [pl.BlockSpec((self.half, self.cols), lambda i, n=n: (0, n)) for n in range(2)] + [row, row],
            [pl.BlockSpec((self.half, tile), lambda i: (0, i))],
            grid=(4,),
        )
        self.dn1_x = swap_x(self.dn1_chip)

    def kv(self):
        own, sent = self.chain.after(self.kv_own, self.kv_from)
        self.kv_chip = (own + sent.astype(F32)).astype(BF16)
        self.kv_x = swap_x(self.kv_chip)

    def kvpart(self):
        chip, from_x = self.chain.after(self.kv_chip, self.kv_x)
        self.d_kv = (chip.astype(F32) + from_x.astype(F32)).astype(BF16)
        mine = lax.dynamic_slice_in_dim(self.d_kv, self.chip * self.head_dim, self.head_dim, 1)
        normed1 = jnp.concatenate(self.normed1, 0)
        part = dot(normed1, mine, TN)
        mine = lax.dynamic_slice_in_dim(part, self.core * self.middle, self.middle, 0)
        other = lax.dynamic_slice_in_dim(part, (1 - self.core) * self.middle, self.middle, 0).astype(BF16)
        self.kv_grad = (mine + swap_core(other).astype(F32)).astype(BF16)

    def out(self):
        chip, from_x = self.chain.after(self.fo_chip, self.fo_x)
        self.output_own = (self.residual + (chip.astype(F32) + from_x.astype(F32))).astype(BF16)
        self.output_sib = swap_core(self.output_own)

    def input(self):
        q, w, d = self.quarter, self.width, 2 * self.head_dim
        self.input_own, self.norm1_part = self.chain.call(
            norm1_back_kernel,
            [shape((self.half, w), BF16), shape((1, w), F32)],
            [self.x, self.dn1_chip, self.dn1_x, self.d_kv, self.kv_w, self.d_residual, self.gain1],
            [
                self.rows(1), self.rows(), self.rows(), pl.BlockSpec((q, d), lambda i, _: (i, 0)),
                whole(self.kv_w), self.rows(), whole(self.gain1),
            ],
            [self.rows(), pl.BlockSpec((1, w), lambda i, _: (0, 0))],
            grid=(2,),
            scalars=[self.own],
        )
        self.input_sib = swap_core(self.input_own)

    def weave_rows(self, own, sibling):
        block = (self.quarter, self.width)
        return self.chain.call(
            weave_kernel,
            [shape((self.length, self.width), BF16)],
            [own, sibling],
            [
                pl.BlockSpec(block, lambda i, _: (jnp.minimum(i, 1), 0)),
                pl.BlockSpec(block, lambda i, _: (jnp.maximum(i - 2, 0), 0)),
            ],
            [pl.BlockSpec(block, lambda i, places: (places[i], 0))],
            grid=(4,),
            scalars=[self.weave_places],
        )[0]

    def weave(self):
        self.block_output = self.weave_rows(self.output_own, self.output_sib)
        self.input_grad = self.weave_rows(self.input_own, self.input_sib)

    def sums(self):
        (parts,) = self.chain.after(jnp.concatenate([self.norm1_part, self.norm2_part], 0))
        self.norm_sums = small_sum(parts, self.n_dp)

    def E(self):
        out_grad = (self.out_mine + self.out_from.astype(F32)).astype(BF16)
        query_grad = (self.query_mine + self.query_from.astype(F32)).astype(BF16)
        self.lanes = self.cols // self.head_dim
        kv_rows = self.middle // self.lanes
        kv_wide = jnp.concatenate([self.kv_grad[i * kv_rows : (i + 1) * kv_rows] for i in range(self.lanes)], 1)
        out_grad, query_grad, kv_wide = self.chain.after(out_grad, query_grad, kv_wide)
        self.kv_sum = empty((8, kv_rows // 8, self.cols), F32)

        def write_out(k, piece):
            self.out_sum = self.place(self.out_sum, piece[None], (k, 0, 0))

        def write_query(k, piece):
            rows = self.width // 8
            self.query_sum = self.place(self.query_sum, piece[None, :rows], (k, 0, 0))
            self.kv_sum = self.place(self.kv_sum, piece[None, rows:], (k, 0, 0))

        self.ring_a.begin(0, [self.eight(out_grad)], write_out)
        self.ring_a.begin(1, [self.eight(query_grad), self.eight(kv_wide)], write_query)

    def a(self):
        self.ring_a.step()

    def b(self):
        self.ring_b.step()

    def results(self):
        d = self.head_dim
        wide = self.kv_sum.reshape(-1, self.cols)
        tall = jnp.concatenate([wide[:, i * d : (i + 1) * d] for i in range(self.lanes)], 0).astype(BF16)
        halves = jnp.stack([tall, swap_core(tall)])
        column = jnp.where(self.core == 0, halves, halves[::-1]).reshape(self.width, d)
        columns = jnp.stack([column, swap_x(column)])
        columns = jnp.where(self.chip == 0, columns, columns[::-1])
        kv_grad = jnp.concatenate([columns[0], columns[1]], 1).astype(F32)
        return (
            self.block_output,
            self.input_grad,
            self.norm_sums[0],
            self.query_sum.reshape(self.width, self.cols),
            kv_grad,
            self.out_sum.reshape(self.cols, self.width),
            self.norm_sums[1],
            self.gate_up_sum.reshape(2, self.width, self.units),
            self.down_sum.reshape(self.units, self.width),
        )


def solution(mesh):
    n_dp = mesh.shape["dp"]

    def local(*args):
        block = Block(n_dp, args)
        for name in ORDER:
            getattr(block, name)()
        return block.results()

    return jax.shard_map(
        local,
        mesh=mesh,
        in_specs=(
            P("dp", None),
            P(),
            P(None, "tensor"),
            P(),
            P("tensor", None),
            P(),
            P(None, None, "tensor"),
            P("tensor", None),
            P("dp", None),
        ),
        out_specs=(
            P("dp", None),
            P("dp", None),
            P(),
            P(None, "tensor"),
            P(),
            P("tensor", None),
            P(),
            P(None, None, "tensor"),
            P("tensor", None),
        ),
        check_vma=False,
    )
```

time: 1270 us -> 477 us (0.38)
  waiting for transfers between devices: 911 us -> 153 us
  matrix products: 140 us -> 0.41 us
  Pallas kernels: 0 us -> 112 us
  starting transfers between devices: 1.17 us -> 104 us
  blocking collectives: 86 us -> 0 us
  other arithmetic: 86.6 us -> 47.3 us
    reduce_scatter x5 -> x0, waiting for transfers between devices: 504 us -> none  [the longest x1 231 us: local(): lax.psum_scatter(gate_up_grad, 'dp', scatter_dimension=1, tiled=True)]
    all_gather x4 -> x0, waiting for transfers between devices: 213 us -> none  [the longest x1 104 us: local(): lax.all_gather(part_gate_up.astype(jnp.bfloat16), 'dp', axis=1, tiled=True)]
    psum x3 -> x0, waiting for transfers between devices: 194 us -> none  [the longest x1 76.4 us: local(): lax.psum(keyvalue_part.astype(jnp.bfloat16), 'tensor').astype(jnp.float32)]
    ppermute x0 -> x108, waiting for transfers between devices: none -> 153 us  [the longest x78 107 us: send(): self.arrived = lax.ppermute(self.travelling, 'dp', self.perm)]
    dot_general x24 -> x1, matrix products: 140 us -> 0.41 us  [dot(): return lax.dot_general(left, right, dims, preferred_element_type=F32)]
    pallas_call x0 -> x29, Pallas kernels: none -> 112 us  [the longest x24 112 us: call(): pl.pallas_call(run, out_shape=outs, grid_spec=pltpu.PrefetchScalarGridSpe...]
    ppermute x0 -> x108, starting transfers between devices: none -> 104 us  [the longest x78 87.5 us: send(): self.arrived = lax.ppermute(self.travelling, 'dp', self.perm)]
    unnamed x2 -> x0, blocking collectives: 52.9 us -> none
  transfers between devices with their start and end apart: 12 -> 108, of which waited for: 11 -> 49; matrix products, arithmetic and copies ran while one was open for 8% -> 11% of each run, Pallas kernels for 0% -> 19%
where the time goes in v2:
time: 477 us; the launch traced here: 469 us
  waiting for transfers between devices  153 us (32%)
  Pallas kernels  112 us (23%)
  starting transfers between devices  104 us (22%)
  other arithmetic  47.3 us (10%)
  local copies, waits for them, and re-layouts  38.7 us (8%)
  between operations  12.9 us (3%)
    pallas_call x24, Pallas kernels, call(): pl.pallas_call(run, out_shape=outs, grid_spec=pltpu.PrefetchScalarGridSpe...  112 us
    ppermute x78, waiting for transfers between devices, send(): self.arrived = lax.ppermute(self.travelling, 'dp', self.perm)  107 us
    ppermute x78, starting transfers between devices, send(): self.arrived = lax.ppermute(self.travelling, 'dp', self.perm)  87.5 us
    dynamic_update_slice x56, other arithmetic, place(): lax.dynamic_update_slice(target, piece.astype(F32), position, allow_negat...  31.6 us
    unnamed x168, local copies, waits for them, and re-layouts  30.8 us
    ppermute x7, waiting for transfers between devices, swap_x(): return lax.ppermute(field, 'tensor', [(i, i ^ 2) for i in range(4)])  27.9 us
    convert_element_type x37, other arithmetic, land(): self.travelling = (self.arrived.astype(F32) + mine.astype(F32)).astype(BF16)  10.7 us
  transfers between devices with their start and end apart: 108, of which 49 were waited for; matrix products, arithmetic and copies ran while one was open for 11% of the time, Pallas kernels for 19%

profile of v2, /device:TPU:0, one launch (start us, length us, event | category | flops | bytes accessed | tf_op | source)
XLA Modules:
  0.0 468.5 jit_solution(8975359722559024823)
XLA Ops:
  9.4 5.4 %shard_map.206 = (bf16[240,1536]{1,0:T(8,128)(2,1)}, bf16[240,768]{1,0:T(8,128)(2,1)S(1)}, bf16[240,768]{1,0:T(8,128)(2,1)S(1)}, f32[240,8]{1,0:T(8,128)S(1)}) custom-call(s32[1]{0:T(128)} %bitcast.refs_0_, bf16[240,1536]{1,0:T(8,128)(2,1)S(1)} %get-tuple-element.190.refs_1_.refs_0_, bf16[960,128]{1,0:T(8,128)(2,1)S(1)} %get-tuple-element.188.refs_2_.refs_9_.refs_6_, ...), custom_call_target="tpu_custom_call" | custom-call | tf_op jit(solution)/shard_map/pallas_call | solution.py:82
  24.6 7.3 %shard_map.207 = (bf16[240,1536]{1,0:T(8,128)(2,1)S(1)}, bf16[240,768]{1,0:T(8,128)(2,1)S(1)}, bf16[240,768]{1,0:T(8,128)(2,1)S(1)}, f32[240,8]{1,0:T(8,128)S(1)}) custom-call(s32[1]{0:T(128)} %bitcast.1.refs_0_, bf16[240,1536]{1,0:T(8,128)(2,1)S(1)} %copy-done.50, bf16[960,128]{1,0:T(8,128)(2,1)S(1)} %copy-done.44, bf16[960,128]{1,0:T(8,128)(2,1)S(1)} %copy-done.55, ...), custom_call_target="tpu_custom_call" | custom-call | tf_op jit(solution)/shard_map/pallas_call | solution.py:82
  35.4 5.4 %shard_map.208 = (bf16[960,1152]{1,0:T(8,128)(2,1)S(1)}, bf16[960,1536]{1,0:T(8,128)(2,1)S(1)}) custom-call(s32[4]{0:T(128)S(1)} %add_add_fusion.1.refs_0_, bf16[960,1536]{1,0:T(8,128)(2,1)S(1)} %copy-done.48, bf16[1152,1536]{1,0:T(8,128)(2,1)S(1)} %copy-done.12, bf16[240,1536]{1,0:T(8,128)(2,1)S(1)} %get-tuple-element.192.refs_3_.refs_2_), custom_call_target="tpu_custom_call" | custom-call | tf_op jit(solution)/shard_map/pallas_call | solution.py:82
  46.5 7.0 %shard_map.210 = (bf16[960,1152]{1,0:T(8,128)(2,1)S(1)}, bf16[960,1152]{1,0:T(8,128)(2,1)S(1)}, bf16[960,1152]{1,0:T(8,128)(2,1)S(1)}, bf16[960,1536]{1,0:T(8,128)(2,1)S(1)}) custom-call(bf16[240,1536]{1,0:T(8,128)(2,1)S(1)} %get-tuple-element.195.refs_0_.refs_4_, bf16[240,1536]{1,0:T(8,128)(2,1)S(1)} %collective-permute-done.4.refs_1_, ...), custom_call_target="tpu_custom_call" | custom-call | tf_op jit(solution)/shard_map/pallas_call | solution.py:82
  53.5 9.5 %collective-permute-done.2.refs_3_ = bf16[240,1536]{1,0:T(8,128)(2,1)S(1)} collective-permute-done((bf16[240,1536]{1,0:T(8,128)(2,1)S(1)}, bf16[240,1536]{1,0:T(8,128)(2,1)S(1)}, u32[]{:S(2)}, u32[]{:S(2)}) %collective-permute-start.2) | collective-permute-done | bytes 737312 | tf_op jit(solution)/shard_map/ppermute | solution.py:60
  78.4 8.2 %shard_map.212 = (bf16[960,1152]{1,0:T(8,128)(2,1)S(1)}, bf16[960,1152]{1,0:T(8,128)(2,1)S(1)}, bf16[960,1152]{1,0:T(8,128)(2,1)S(1)}, bf16[960,1536]{1,0:T(8,128)(2,1)S(1)}) custom-call(bf16[240,1536]{1,0:T(8,128)(2,1)} %get-tuple-element.198.refs_0_.refs_8_, ...), custom_call_target="tpu_custom_call", output_to_operand_aliasing={{0}: (4, {}), {1}: (5, {}), {2}: (6, {}), {3}: (7, {})} | custom-call | tf_op jit(solution)/shard_map/pallas_call | solution.py:82
  101.5 4.9 %shard_map.215.refs_2_ = bf16[1536,1152]{1,0:T(8,128)(2,1)S(1)} custom-call(bf16[960,1536]{1,0:T(8,128)(2,1)S(1)} %get-tuple-element.208.refs_0_, bf16[960,1152]{1,0:T(8,128)(2,1)S(1)} %get-tuple-element.205.refs_1_, bf16[1152,768]{1,0:T(8,128)(2,1)S(1)} %shard_map.214.refs_2_), custom_call_target="tpu_custom_call" | custom-call | tf_op jit(solution)/shard_map/pallas_call | solution.py:82
  110.4 4.9 %shard_map.216.refs_4_ = bf16[1536,1152]{1,0:T(8,128)(2,1)S(1)} custom-call(bf16[960,1536]{1,0:T(8,128)(2,1)S(1)} %get-tuple-element.208.refs_0_, bf16[960,1152]{1,0:T(8,128)(2,1)S(1)} %copy-done.11, bf16[1536,1152]{1,0:T(8,128)(2,1)S(1)} %shard_map.215.refs_2_, bf16[144,768]{1,0:T(8,128)(2,1)S(1)} %fusion.31.refs_3_, bf16[144,768]{1,0:T(8,128)(2,1)S(1)} %fusion.30.refs_4_), custom_call_target="tpu_custom_call" | custom-call | tf_op jit(solution)/shard_map/pallas_call | solution.py:82
  117.6 5.9 %shard_map.217.refs_5_ = bf16[480,1536]{1,0:T(8,128)(2,1)S(1)} custom-call(bf16[2,2,240,1152]{3,2,1,0:T(8,128)(2,1)S(1)} %bitcast.377, bf16[2,2,240,1152]{3,2,1,0:T(8,128)(2,1)S(1)} %bitcast.379, bf16[2,1536,1152]{2,1,0:T(8,128)(2,1)S(1)} %bitcast.374, bf16[2,1536,1152]{2,1,0:T(8,128)(2,1)S(1)} %bitcast.374, bf16[1536,1152]{1,0:T(8,128)(2,1)S(1)} %shard_map.216.refs_4_, ...), custom_call_target="tpu_custom_call" | custom-call | tf_op jit(solution)/shard_map/pallas_call | solution.py:82
  124.8 3.2 collective-permute-done.13
  130.3 6.4 %collective-permute-done.12 = bf16[192,1152]{1,0:T(8,128)(2,1)S(1)} collective-permute-done((bf16[192,1152]{1,0:T(8,128)(2,1)S(1)}, bf16[192,1152]{1,0:T(8,128)(2,1)S(1)}, u32[]{:S(2)}, u32[]{:S(2)}) %collective-permute-start.12) | collective-permute-done | bytes 442400 | tf_op jit(solution)/shard_map/ppermute | solution.py:387
  139.1 6.1 %shard_map.218.refs_1_.refs_7_ = bf16[480,1536]{1,0:T(8,128)(2,1)S(1)} custom-call(bf16[2,2,240,1152]{3,2,1,0:T(8,128)(2,1)S(1)} %bitcast.378, bf16[2,2,240,1152]{3,2,1,0:T(8,128)(2,1)S(1)} %bitcast.380, bf16[2,1536,1152]{2,1,0:T(8,128)(2,1)S(1)} %bitcast.374, bf16[2,1536,1152]{2,1,0:T(8,128)(2,1)S(1)} %bitcast.374, ...), custom_call_target="tpu_custom_call" | custom-call | tf_op jit(solution)/shard_map/pallas_call | solution.py:82
  169.4 5.4 %collective-permute-done.26 = bf16[192,1152]{1,0:T(8,128)(2,1)S(1)} collective-permute-done((bf16[192,1152]{1,0:T(8,128)(2,1)}, bf16[192,1152]{1,0:T(8,128)(2,1)S(1)}, u32[]{:S(2)}, u32[]{:S(2)}) %collective-permute-start.26) | collective-permute-done | bytes 442400 | tf_op jit(solution)/shard_map/ppermute | solution.py:400
  186.5 7.8 %collective-permute-done.15.refs_2_ = bf16[480,1536]{1,0:T(8,128)(2,1)S(1)} collective-permute-done((bf16[480,1536]{1,0:T(8,128)(2,1)}, bf16[480,1536]{1,0:T(8,128)(2,1)S(1)}, u32[]{:S(2)}, u32[]{:S(2)}) %collective-permute-start.15) | collective-permute-done | bytes 1474592 | tf_op jit(solution)/shard_map/ppermute | solution.py:60
  195.7 4.7 %shard_map.219 = (f32[480,1536]{1,0:T(8,128)S(1)}, bf16[480,1536]{1,0:T(8,128)(2,1)S(1)}, bf16[480,768]{1,0:T(8,128)(2,1)S(1)}, f32[1,1536]{1,0:T(1,128)S(1)}) custom-call(f32[480,1536]{1,0:T(8,128)S(1)} %copy-done.19, bf16[480,1536]{1,0:T(8,128)(2,1)S(1)} %copy-done.31, bf16[480,1536]{1,0:T(8,128)(2,1)S(1)} %collective-permute-done.15.refs_2_, ...), custom_call_target="tpu_custom_call" | custom-call | tf_op jit(solution)/shard_map/pallas_call | solution.py:82
  200.5 14.4 %shard_map.220 = (bf16[480,768]{1,0:T(8,128)(2,1)S(1)}, f32[480,256]{1,0:T(8,128)S(1)}, bf16[480,256]{1,0:T(8,128)(2,1)S(1)}) custom-call(s32[1]{0:T(128)} %bitcast.refs_0_, bf16[240,768]{1,0:T(8,128)(2,1)S(1)} %copy-done.62, bf16[240,768]{1,0:T(8,128)(2,1)S(1)} %copy-done.64, f32[240,8]{1,0:T(8,128)S(1)} %get-tuple-element.242.refs_3_, ...), custom_call_target="tpu_custom_call" | custom-call | tf_op jit(solution)/shard_map/pallas_call | solution.py:82
  228.6 4.1 collective-permute-done.38
  244.8 6.5 %collective-permute-done.45 = bf16[144,768]{1,0:T(8,128)(2,1)S(1)} collective-permute-done((bf16[144,768]{1,0:T(8,128)(2,1)S(1)}, bf16[144,768]{1,0:T(8,128)(2,1)S(1)}, u32[]{:S(2)}, u32[]{:S(2)}) %collective-permute-start.45) | collective-permute-done | bytes 221216 | tf_op jit(solution)/shard_map/ppermute | solution.py:400
  260.2 4.7 %shard_map.223.refs_2_ = bf16[480,1536]{1,0:T(8,128)(2,1)} custom-call(bf16[480,768]{1,0:T(8,128)(2,1)S(1)} %get-tuple-element.252.refs_2_.refs_3_.refs_0_.refs_1_, bf16[480,768]{1,0:T(8,128)(2,1)S(1)} %get-tuple-element.252.refs_2_.refs_3_.refs_0_.refs_1_, bf16[1536,384]{1,0:T(8,128)(2,1)S(1)} %copy-done.38, ...), custom_call_target="tpu_custom_call" | custom-call | tf_op jit(solution)/shard_map/pallas_call | solution.py:82
  272.8 5.1 %collective-permute-done.48 = bf16[192,1152]{1,0:T(8,128)(2,1)S(1)} collective-permute-done((bf16[192,1152]{1,0:T(8,128)(2,1)S(1)}, bf16[192,1152]{1,0:T(8,128)(2,1)S(1)}, u32[]{:S(2)}, u32[]{:S(2)}) %collective-permute-start.48) | collective-permute-done | bytes 442400 | tf_op jit(solution)/shard_map/ppermute | solution.py:400
  285.7 7.6 %collective-permute-done.55 = bf16[144,768]{1,0:T(8,128)(2,1)S(1)} collective-permute-done((bf16[144,768]{1,0:T(8,128)(2,1)S(1)}, bf16[144,768]{1,0:T(8,128)(2,1)S(1)}, u32[]{:S(2)}, u32[]{:S(2)}) %collective-permute-start.55) | collective-permute-done | bytes 221216 | tf_op jit(solution)/shard_map/ppermute | solution.py:400
  308.0 3.7 shard_map.224.refs_3_
  326.6 3.9 shard_map.225.refs_8_
  333.7 4.0 collective-permute-done.69
  354.3 4.2 collective-permute-done.75
  362.6 3.9 shard_map.226
  377.4 4.6 collective-permute-done.88
  389.1 7.5 %collective-permute-done.83 = bf16[192,1152]{1,0:T(8,128)(2,1)S(1)} collective-permute-done((bf16[192,1152]{1,0:T(8,128)(2,1)S(1)}, bf16[192,1152]{1,0:T(8,128)(2,1)S(1)}, u32[]{:S(2)}, u32[]{:S(2)}) %collective-permute-start.83) | collective-permute-done | bytes 442400 | tf_op jit(solution)/shard_map/ppermute | solution.py:400
  425.0 8.5 %collective-permute-done.96 = bf16[48,1536]{1,0:T(8,128)(2,1)S(1)} collective-permute-done((bf16[48,1536]{1,0:T(8,128)(2,1)S(1)}, bf16[48,1536]{1,0:T(8,128)(2,1)S(1)}, u32[]{:S(2)}, u32[]{:S(2)}) %collective-permute-start.96) | collective-permute-done | bytes 147488 | tf_op jit(solution)/shard_map/ppermute | solution.py:400
  444.6 3.6 collective-permute-done.102
  450.3 3.2 collective-permute-done.104
  455.9 10.6 %collective-permute-done.107 = bf16[1536,128]{1,0:T(8,128)(2,1)S(1)} collective-permute-done((bf16[1536,128]{1,0:T(8,128)(2,1)S(1)}, bf16[1536,128]{1,0:T(8,128)(2,1)S(1)}, u32[]{:S(2)}, u32[]{:S(2)}) %collective-permute-start.107) | collective-permute-done | bytes 393248 | tf_op jit(solution)/shard_map/ppermute | solution.py:60
  (516 shorter events, 263.2 us)
Async XLA Ops:
  16.3 24.5 %collective-permute-start.3 = (bf16[240,1536]{1,0:T(8,128)(2,1)}, bf16[240,1536]{1,0:T(8,128)(2,1)}, u32[]{:S(2)}, u32[]{:S(2)}) collective-permute-start(bf16[240,1536]{1,0:T(8,128)(2,1)} %get-tuple-element.191.refs_9_.refs_2_), channel_id=1, source_target_pairs={{0,2},{1,3},{2,0},{3,1},{4,6},{5,7},{6,4},{7,5},{8,10},{9,11},{10,... | collective-permute-start | bytes 2211848 | tf_op jit(solution)/shard_map/ppermute | solution.py:60
  44.6 18.5 %collective-permute-start.2 = (bf16[240,1536]{1,0:T(8,128)(2,1)S(1)}, bf16[240,1536]{1,0:T(8,128)(2,1)S(1)}, u32[]{:S(2)}, u32[]{:S(2)}) collective-permute-start(bf16[240,1536]{1,0:T(8,128)(2,1)S(1)} %get-tuple-element.192.refs_3_.refs_2_), channel_id=1, source_target_pairs={{0,2},{1,3},{2,0},{3,1},{4,6},{5,7},{6,4},{7,5},{8,10},{9,11},{10,... | collective-permute-start | bytes 2211848 | tf_op jit(solution)/shard_map/ppermute | solution.py:60
  108.8 21.5 %collective-permute-start.11 = (bf16[192,1152]{1,0:T(8,128)(2,1)S(1)}, bf16[192,1152]{1,0:T(8,128)(2,1)S(1)}, u32[]{:S(2)}, u32[]{:S(2)}) collective-permute-start(bf16[192,1152]{1,0:T(8,128)(2,1)S(1)} %dynamic-slice_bitcast_fusion.1), channel_id=1, source_target_pairs={{0,8},{8,16},{16,24},{24,28},{28,20},{20,12},{12,4},{4,0},{1,9},{9... | collective-permute-start | bytes 1327112 | tf_op jit(solution)/shard_map/ppermute | solution.py:387
  123.6 15.5 %collective-permute-start.10 = (bf16[480,1536]{1,0:T(8,128)(2,1)S(1)}, bf16[480,1536]{1,0:T(8,128)(2,1)S(1)}, u32[]{:S(2)}, u32[]{:S(2)}) collective-permute-start(bf16[480,1536]{1,0:T(8,128)(2,1)S(1)} %shard_map.217.refs_5_), channel_id=1, source_target_pairs={{0,1},{1,0},{2,3},{3,2},{4,5},{5,4},{6,7},{7,6},{8,9},{9,8},{10,11... | collective-permute-start | bytes 4423688 | tf_op jit(solution)/shard_map/ppermute | solution.py:56
  128.1 17.1 %collective-permute-start.16 = (bf16[144,768]{1,0:T(8,128)(2,1)S(1)}, bf16[144,768]{1,0:T(8,128)(2,1)S(1)}, u32[]{:S(2)}, u32[]{:S(2)}) collective-permute-start(bf16[144,768]{1,0:T(8,128)(2,1)S(1)} %fusion.27), channel_id=1, source_target_pairs={{0,8},{8,16},{16,24},{24,28},{28,20},{20,12},{12,4},{4,0},{1,9},{9... | collective-permute-start | bytes 663560 | tf_op jit(solution)/shard_map/ppermute | solution.py:400
  129.8 15.4 %collective-permute-start.17 = (bf16[144,768]{1,0:T(8,128)(2,1)S(1)}, bf16[144,768]{1,0:T(8,128)(2,1)S(1)}, u32[]{:S(2)}, u32[]{:S(2)}) collective-permute-start(bf16[144,768]{1,0:T(8,128)(2,1)S(1)} %fusion.26), channel_id=1, source_target_pairs={{4,12},{12,20},{20,28},{28,24},{24,16},{16,8},{8,0},{0,4},{5,13},{... | collective-permute-start | bytes 663560 | tf_op jit(solution)/shard_map/ppermute | solution.py:400
  161.4 32.8 %collective-permute-start.15 = (bf16[480,1536]{1,0:T(8,128)(2,1)}, bf16[480,1536]{1,0:T(8,128)(2,1)S(1)}, u32[]{:S(2)}, u32[]{:S(2)}) collective-permute-start(bf16[480,1536]{1,0:T(8,128)(2,1)} %copy-done.30), channel_id=1, source_target_pairs={{0,2},{1,3},{2,0},{3,1},{4,6},{5,7},{6,4},{7,5},{8,10},{9,11},{10,... | collective-permute-start | bytes 4423688 | tf_op jit(solution)/shard_map/ppermute | solution.py:60
  166.2 14.6 %collective-permute-start.24 = (bf16[144,768]{1,0:T(8,128)(2,1)S(1)}, bf16[144,768]{1,0:T(8,128)(2,1)S(1)}, u32[]{:S(2)}, u32[]{:S(2)}) collective-permute-start(bf16[144,768]{1,0:T(8,128)(2,1)S(1)} %fusion.21), channel_id=1, source_target_pairs={{0,8},{8,16},{16,24},{24,28},{28,20},{20,12},{12,4},{4,0},{1,9},{9... | collective-permute-start | bytes 663560 | tf_op jit(solution)/shard_map/ppermute | solution.py:400
  178.7 38.4 %collective-permute-start.33 = (bf16[192,1152]{1,0:T(8,128)(2,1)S(1)}, bf16[192,1152]{1,0:T(8,128)(2,1)S(1)}, u32[]{:S(2)}, u32[]{:S(2)}) collective-permute-start(bf16[192,1152]{1,0:T(8,128)(2,1)S(1)} %fusion.13), channel_id=1, source_target_pairs={{0,8},{8,16},{16,24},{24,28},{28,20},{20,12},{12,4},{4,0},{1,9},{9... | collective-permute-start | bytes 1327112 | tf_op jit(solution)/shard_map/ppermute | solution.py:400
  180.6 36.5 %collective-permute-start.34 = (bf16[192,1152]{1,0:T(8,128)(2,1)S(1)}, bf16[192,1152]{1,0:T(8,128)(2,1)S(1)}, u32[]{:S(2)}, u32[]{:S(2)}) collective-permute-start(bf16[192,1152]{1,0:T(8,128)(2,1)S(1)} %fusion.12), channel_id=1, source_target_pairs={{4,12},{12,20},{20,28},{28,24},{24,16},{16,8},{8,0},{0,4},{5,13},{... | collective-permute-start | bytes 1327112 | tf_op jit(solution)/shard_map/ppermute | solution.py:400
  182.5 32.5 %collective-permute-start.29 = (bf16[144,768]{1,0:T(8,128)(2,1)S(1)}, bf16[144,768]{1,0:T(8,128)(2,1)S(1)}, u32[]{:S(2)}, u32[]{:S(2)}) collective-permute-start(bf16[144,768]{1,0:T(8,128)(2,1)S(1)} %get-tuple-element.370.refs_8_), channel_id=1, source_target_pairs={{0,8},{8,16},{16,24},{24,28},{28,20},{20,12},{12,4},{4,0},{1,9},{9... | collective-permute-start | bytes 663560 | tf_op jit(solution)/shard_map/ppermute | solution.py:400
  186.1 28.9 %collective-permute-start.30 = (bf16[144,768]{1,0:T(8,128)(2,1)S(1)}, bf16[144,768]{1,0:T(8,128)(2,1)S(1)}, u32[]{:S(2)}, u32[]{:S(2)}) collective-permute-start(bf16[144,768]{1,0:T(8,128)(2,1)S(1)} %get-tuple-element.368.refs_9_), channel_id=1, source_target_pairs={{4,12},{12,20},{20,28},{28,24},{24,16},{16,8},{8,0},{0,4},{5,13},{... | collective-permute-start | bytes 663560 | tf_op jit(solution)/shard_map/ppermute | solution.py:400
  217.4 15.4 %collective-permute-start.38 = (bf16[192,1152]{1,0:T(8,128)(2,1)S(1)}, bf16[192,1152]{1,0:T(8,128)(2,1)S(1)}, u32[]{:S(2)}, u32[]{:S(2)}) collective-permute-start(bf16[192,1152]{1,0:T(8,128)(2,1)S(1)} %fusion.11.refs_4_), channel_id=1, source_target_pairs={{0,8},{8,16},{16,24},{24,28},{28,20},{20,12},{12,4},{4,0},{1,9},{9... | collective-permute-start | bytes 1327112 | tf_op jit(solution)/shard_map/ppermute | solution.py:400
  219.0 15.4 %collective-permute-start.39 = (bf16[192,1152]{1,0:T(8,128)(2,1)S(1)}, bf16[192,1152]{1,0:T(8,128)(2,1)S(1)}, u32[]{:S(2)}, u32[]{:S(2)}) collective-permute-start(bf16[192,1152]{1,0:T(8,128)(2,1)S(1)} %fusion.10.refs_5_), channel_id=1, source_target_pairs={{4,12},{12,20},{20,28},{28,24},{24,16},{16,8},{8,0},{0,4},{5,13},{... | collective-permute-start | bytes 1327112 | tf_op jit(solution)/shard_map/ppermute | solution.py:400
  223.3 45.2 %collective-permute-start.41 = (bf16[1536,384]{1,0:T(8,128)(2,1)S(1)}, bf16[1536,384]{1,0:T(8,128)(2,1)S(1)}, u32[]{:S(2)}, u32[]{:S(2)}) collective-permute-start(bf16[1536,384]{1,0:T(8,128)(2,1)S(1)} %get-tuple-element.273), channel_id=1, source_target_pairs={{0,1},{1,0},{2,3},{3,2},{4,5},{5,4},{6,7},{7,6},{8,9},{9,8},{10,11... | collective-permute-start | bytes 3538952 | tf_op jit(solution)/shard_map/ppermute | solution.py:56
  234.7 22.9 %collective-permute-start.43 = (bf16[192,1152]{1,0:T(8,128)(2,1)S(1)}, bf16[192,1152]{1,0:T(8,128)(2,1)S(1)}, u32[]{:S(2)}, u32[]{:S(2)}) collective-permute-start(bf16[192,1152]{1,0:T(8,128)(2,1)S(1)} %fusion.9), channel_id=1, source_target_pairs={{0,8},{8,16},{16,24},{24,28},{28,20},{20,12},{12,4},{4,0},{1,9},{9... | collective-permute-start | bytes 1327112 | tf_op jit(solution)/shard_map/ppermute | solution.py:400
  237.5 20.4 %collective-permute-start.44 = (bf16[192,1152]{1,0:T(8,128)(2,1)S(1)}, bf16[192,1152]{1,0:T(8,128)(2,1)S(1)}, u32[]{:S(2)}, u32[]{:S(2)}) collective-permute-start(bf16[192,1152]{1,0:T(8,128)(2,1)S(1)} %fusion.8), channel_id=1, source_target_pairs={{4,12},{12,20},{20,28},{28,24},{24,16},{16,8},{8,0},{0,4},{5,13},{... | collective-permute-start | bytes 1327112 | tf_op jit(solution)/shard_map/ppermute | solution.py:400
  251.3 44.5 %collective-permute-start.40 = (bf16[384,1536]{1,0:T(8,128)(2,1)S(1)}, bf16[384,1536]{1,0:T(8,128)(2,1)S(1)}, u32[]{:S(2)}, u32[]{:S(2)}) collective-permute-start(bf16[384,1536]{1,0:T(8,128)(2,1)S(1)} %get-tuple-element.272), channel_id=1, source_target_pairs={{0,1},{1,0},{2,3},{3,2},{4,5},{5,4},{6,7},{7,6},{8,9},{9,8},{10,11... | collective-permute-start | bytes 3538952 | tf_op jit(solution)/shard_map/ppermute | solution.py:56
  258.0 14.8 %collective-permute-start.47 = (bf16[192,1152]{1,0:T(8,128)(2,1)S(1)}, bf16[192,1152]{1,0:T(8,128)(2,1)S(1)}, u32[]{:S(2)}, u32[]{:S(2)}) collective-permute-start(bf16[192,1152]{1,0:T(8,128)(2,1)S(1)} %fusion.7.refs_5_), channel_id=1, source_target_pairs={{0,8},{8,16},{16,24},{24,28},{28,20},{20,12},{12,4},{4,0},{1,9},{9... | collective-permute-start | bytes 1327112 | tf_op jit(solution)/shard_map/ppermute | solution.py:400
  265.2 16.8 %collective-permute-start.53 = (bf16[144,768]{1,0:T(8,128)(2,1)S(1)}, bf16[144,768]{1,0:T(8,128)(2,1)S(1)}, u32[]{:S(2)}, u32[]{:S(2)}) collective-permute-start(bf16[144,768]{1,0:T(8,128)(2,1)S(1)} %collective-permute-done.49), channel_id=1, source_target_pairs={{0,8},{8,16},{16,24},{24,28},{28,20},{20,12},{12,4},{4,0},{1,9},{9... | collective-permute-start | bytes 663560 | tf_op jit(solution)/shard_map/ppermute | solution.py:400
  279.0 17.1 %collective-permute-start.51 = (bf16[192,1152]{1,0:T(8,128)(2,1)S(1)}, bf16[192,1152]{1,0:T(8,128)(2,1)S(1)}, u32[]{:S(2)}, u32[]{:S(2)}) collective-permute-start(bf16[192,1152]{1,0:T(8,128)(2,1)S(1)} %get-tuple-element.374), channel_id=1, source_target_pairs={{0,8},{8,16},{16,24},{24,28},{28,20},{20,12},{12,4},{4,0},{1,9},{9... | collective-permute-start | bytes 1327112 | tf_op jit(solution)/shard_map/ppermute | solution.py:400
  281.8 14.3 %collective-permute-start.52 = (bf16[192,1152]{1,0:T(8,128)(2,1)S(1)}, bf16[192,1152]{1,0:T(8,128)(2,1)S(1)}, u32[]{:S(2)}, u32[]{:S(2)}) collective-permute-start(bf16[192,1152]{1,0:T(8,128)(2,1)S(1)} %get-tuple-element.372), channel_id=1, source_target_pairs={{4,12},{12,20},{20,28},{28,24},{24,16},{16,8},{8,0},{0,4},{5,13},{... | collective-permute-start | bytes 1327112 | tf_op jit(solution)/shard_map/ppermute | solution.py:400
  297.8 14.0 %collective-permute-start.58 = (bf16[48,1536]{1,0:T(8,128)(2,1)}, bf16[48,1536]{1,0:T(8,128)(2,1)}, u32[]{:S(2)}, u32[]{:S(2)}) collective-permute-start(bf16[48,1536]{1,0:T(8,128)(2,1)} %dynamic-slice_bitcast_fusion.12), channel_id=1, source_target_pairs={{0,8},{8,16},{16,24},{24,28},{28,20},{20,12},{12,4},{4,0},{1,9},{9... | collective-permute-start | bytes 442376 | tf_op jit(solution)/shard_map/ppermute | solution.py:387
  311.7 14.6 %collective-permute-start.57 = (bf16[480,1536]{1,0:T(8,128)(2,1)S(1)}, bf16[480,1536]{1,0:T(8,128)(2,1)S(1)}, u32[]{:S(2)}, u32[]{:S(2)}) collective-permute-start(bf16[480,1536]{1,0:T(8,128)(2,1)S(1)} %shard_map.224.refs_3_), channel_id=1, source_target_pairs={{0,1},{1,0},{2,3},{3,2},{4,5},{5,4},{6,7},{7,6},{8,9},{9,8},{10,11... | collective-permute-start | bytes 4423688 | tf_op jit(solution)/shard_map/ppermute | solution.py:56
  315.8 46.8 %collective-permute-start.79 = (bf16[480,1536]{1,0:T(8,128)(2,1)}, bf16[480,1536]{1,0:T(8,128)(2,1)S(1)}, u32[]{:S(2)}, u32[]{:S(2)}) collective-permute-start(bf16[480,1536]{1,0:T(8,128)(2,1)} %shard_map.223.refs_2_), channel_id=1, source_target_pairs={{0,2},{1,3},{2,0},{3,1},{4,6},{5,7},{6,4},{7,5},{8,10},{9,11},{10,... | collective-permute-start | bytes 4423688 | tf_op jit(solution)/shard_map/ppermute | solution.py:60
  358.5 43.6 %collective-permute-start.64 = (bf16[480,1536]{1,0:T(8,128)(2,1)S(1)}, bf16[480,1536]{1,0:T(8,128)(2,1)S(1)}, u32[]{:S(2)}, u32[]{:S(2)}) collective-permute-start(bf16[480,1536]{1,0:T(8,128)(2,1)S(1)} %shard_map.225.refs_8_), channel_id=1, source_target_pairs={{0,2},{1,3},{2,0},{3,1},{4,6},{5,7},{6,4},{7,5},{8,10},{9,11},{10,... | collective-permute-start | bytes 4423688 | tf_op jit(solution)/shard_map/ppermute | solution.py:60
  371.8 17.3 %collective-permute-start.82 = (bf16[192,1152]{1,0:T(8,128)(2,1)S(1)}, bf16[192,1152]{1,0:T(8,128)(2,1)S(1)}, u32[]{:S(2)}, u32[]{:S(2)}) collective-permute-start(bf16[192,1152]{1,0:T(8,128)(2,1)S(1)} %collective-permute-done.75), channel_id=1, source_target_pairs={{0,8},{8,16},{16,24},{24,28},{28,20},{20,12},{12,4},{4,0},{1,9},{9... | collective-permute-start | bytes 1327112 | tf_op jit(solution)/shard_map/ppermute | solution.py:400
  389.1 21.7 %collective-permute-start.85 = (bf16[480,1536]{1,0:T(8,128)(2,1)S(1)}, bf16[480,1536]{1,0:T(8,128)(2,1)S(1)}, u32[]{:S(2)}, u32[]{:S(2)}) collective-permute-start(bf16[480,1536]{1,0:T(8,128)(2,1)S(1)} %get-tuple-element.345.refs_3_.refs_1_), channel_id=1, source_target_pairs={{0,1},{1,0},{2,3},{3,2},{4,5},{5,4},{6,7},{7,6},{8,9},{9,8},{10,11... | collective-permute-start | bytes 4423688 | tf_op jit(solution)/shard_map/ppermute | solution.py:56
  396.6 21.0 %collective-permute-start.94 = (bf16[192,1152]{1,0:T(8,128)(2,1)S(1)}, bf16[192,1152]{1,0:T(8,128)(2,1)S(1)}, u32[]{:S(2)}, u32[]{:S(2)}) collective-permute-start(bf16[192,1152]{1,0:T(8,128)(2,1)S(1)} %collective-permute-done.82), channel_id=1, source_target_pairs={{0,8},{8,16},{16,24},{24,28},{28,20},{20,12},{12,4},{4,0},{1,9},{9... | collective-permute-start | bytes 1327112 | tf_op jit(solution)/shard_map/ppermute | solution.py:400
  399.7 15.6 %collective-permute-start.90 = (bf16[48,1536]{1,0:T(8,128)(2,1)S(1)}, bf16[48,1536]{1,0:T(8,128)(2,1)S(1)}, u32[]{:S(2)}, u32[]{:S(2)}) collective-permute-start(bf16[48,1536]{1,0:T(8,128)(2,1)S(1)} %collective-permute-done.80.refs_4_), channel_id=1, source_target_pairs={{0,8},{8,16},{16,24},{24,28},{28,20},{20,12},{12,4},{4,0},{1,9},{9... | collective-permute-start | bytes 442376 | tf_op jit(solution)/shard_map/ppermute | solution.py:400
  418.5 18.8 %collective-permute-start.100 = (bf16[192,1152]{1,0:T(8,128)(2,1)S(1)}, bf16[192,1152]{1,0:T(8,128)(2,1)S(1)}, u32[]{:S(2)}, u32[]{:S(2)}) collective-permute-start(bf16[192,1152]{1,0:T(8,128)(2,1)S(1)} %collective-permute-done.94), channel_id=1, source_target_pairs={{0,8},{8,16},{16,24},{24,28},{28,20},{20,12},{12,4},{4,0},{1,9},{9... | collective-permute-start | bytes 1327112 | tf_op jit(solution)/shard_map/ppermute | solution.py:400
  420.3 17.0 %collective-permute-start.101 = (bf16[192,1152]{1,0:T(8,128)(2,1)S(1)}, bf16[192,1152]{1,0:T(8,128)(2,1)S(1)}, u32[]{:S(2)}, u32[]{:S(2)}) collective-permute-start(bf16[192,1152]{1,0:T(8,128)(2,1)S(1)} %collective-permute-done.95), channel_id=1, source_target_pairs={{4,12},{12,20},{20,28},{28,24},{24,16},{16,8},{8,0},{0,4},{5,13},{... | collective-permute-start | bytes 1327112 | tf_op jit(solution)/shard_map/ppermute | solution.py:400
  (160 other events, 1612.8 us)
